TPU v7x, 512 devices: a whole 4x4x16 slice. The times are simulated.
512 devices in a mesh: ja: 16 (over y_hi, x, core), ia: 32 (over z, y_lo).
Axes of the slice: x: 4, y: 4 (y_hi: 2, y_lo: 2; y = y_hi * 2 + y_lo), z: 16, core: 2. Of those that a mesh axis runs over, the one named last changes fastest.
Arguments:
- potential_warmth: float32 [16, 1024, 4096], P(None, 'ja', 'ia'), may hold values from -2 to 30
- saltiness_psu: float32 [16, 1024, 4096], P(None, 'ja', 'ia'), may hold values from 33 to 37
- zonal_stability_ratio: float32 [16, 1024, 4096], P(None, 'ja', 'ia'), may hold values from -0.3 to 0.3
- poleward_stability_ratio: float32 [16, 1024, 4096], P(None, 'ja', 'ia'), may hold values from -0.3 to 0.3
- sinking_stability_ratio: float32 [16, 1024, 4096], P(None, 'ja', 'ia'), may hold values from -0.2 to 0.2
- seafloor_layer_index: int32 [1024, 4096], P('ja', 'ia'), may hold values from 0 to 16, as said below
Outputs:
- temperature_next: float32 [16, 1024, 4096], P(None, 'ja', 'ia')
- salinity_next: float32 [16, 1024, 4096], P(None, 'ja', 'ia')
Inputs may be any that keep to these rules, and one draw needn't show every extreme that they name: Dry columns hold 0; a column is wet from the surface down to level seafloor_layer_index - 1; dry columns come in blocks of 32 rows by 64 columns.
All inputs are finite; a program needn't handle non-finite values.
Results may differ from a plain program's by a relative error of at most 0.0003.
Values sent between devices are 32-bit elements; how exact they have to be, the bound alone decides.
No kernel may reach another device: no remote copies, remote signals or barrier semaphores. Data moves between devices by JAX's collectives and lax.ppermute only.
A program may use at most 128 MiB of HBM per device.

v0:
```python
import jax
import jax.numpy as jnp
from jax import lax
from jax.sharding import PartitionSpec as P

THERMAL_COEF = 0.1655
HALINE_COEF = 0.76554
CABBELING_T = 0.05952
CABBELING_S = 0.00054914
THERMOBARIC_T = 0.0001497
THERMOBARIC_S = 1.109e-05
MIXED_COEF = 0.0024341
LAYER_DEPTH = 50.0
MIXING_BASE = 0.5
MIXING_CONV = 10.0
DENSITY_SCALE = 0.5


def padded_2(cells, sides, width, closed):
    for axis, dim in sides:
        count = lax.axis_size(axis)
        ends = count if closed else count - 1
        head = lax.slice_in_dim(cells, 0, width, axis=dim)
        tail = lax.slice_in_dim(cells, cells.shape[dim] - width, cells.shape[dim], axis=dim)
        cells = jnp.concatenate(
            [
                lax.ppermute(tail, axis, [(i, (i + 1) % count) for i in range(ends)]),
                cells,
                lax.ppermute(head, axis, [((i + 1) % count, i) for i in range(ends)]),
            ],
            axis=dim,
        )
    return cells


def partner(x, axis, apart):
    return lax.ppermute(x, axis, [(i, i ^ 1 << apart) for i in range(lax.axis_size(axis))])


def take_slab(array, offset, length, along):
    return lax.slice_in_dim(array, offset, offset + length, axis=along % array.ndim)


def min_modulus(left_slope, right_slope):
    return (
        0.5
        * (jnp.sign(left_slope) + jnp.sign(right_slope))
        * jnp.minimum(jnp.abs(left_slope), jnp.abs(right_slope))
    )


def tvd_divergence(scalar_quantity, seawater_indicator, stability_ratio, along):
    count = scalar_quantity.shape[along % scalar_quantity.ndim] - 4
    face_wet = take_slab(seawater_indicator, 0, count + 3, along) * take_slab(
        seawater_indicator, 1, count + 3, along
    )
    slopes = face_wet * (
        take_slab(scalar_quantity, 1, count + 3, along)
        - take_slab(scalar_quantity, 0, count + 3, along)
    )
    centre = take_slab(slopes, 1, count + 1, along)
    below_face = take_slab(slopes, 0, count + 1, along)
    above_face = take_slab(slopes, 2, count + 1, along)
    open_face = take_slab(face_wet, 1, count + 1, along)
    upwind_left = take_slab(scalar_quantity, 1, count + 1, along)
    upwind_right = take_slab(scalar_quantity, 2, count + 1, along)
    damping = 0.5 * (1.0 - jnp.abs(stability_ratio))
    face_value = jnp.where(
        stability_ratio > 0,
        upwind_left + damping * min_modulus(centre, below_face),
        upwind_right - damping * min_modulus(centre, above_face),
    )
    flux = stability_ratio * open_face * face_value
    return take_slab(flux, 1, count, along) - take_slab(flux, 0, count, along)


def density(temp_star, salt_star, depth):
    anomaly_t = temp_star - 10.0
    anomaly_s = salt_star - 35.0
    return (
        -THERMAL_COEF * (1.0 + 0.5 * CABBELING_T * anomaly_t + THERMOBARIC_T * depth) * anomaly_t
        + HALINE_COEF * (1.0 - 0.5 * CABBELING_S * anomaly_s - THERMOBARIC_S * depth) * anomaly_s
        - MIXED_COEF * anomaly_t * anomaly_s
    )


def column_mixing_physics(scalar_quantities, horizontal_part, down_faces, seawater_indicator):
    layer_total = scalar_quantities.shape[1]
    depth = (LAYER_DEPTH * (jnp.arange(layer_total, dtype=jnp.float32) + 0.5))[:, None, None]
    padded = jnp.pad(scalar_quantities, ((0, 0), (2, 2), (0, 0), (0, 0)))
    wet_padded = jnp.pad(seawater_indicator, ((2, 2), (0, 0), (0, 0)))
    faces = jnp.pad(down_faces[:-1], ((1, 1), (0, 0), (0, 0)))
    vertical = tvd_divergence(padded, wet_padded, faces, -3)
    star = seawater_indicator * (scalar_quantities - horizontal_part - vertical)
    density_now = density(star[0], star[1], depth)
    density_jump = density_now[1:] - density_now[:-1]
    mixing = (
        seawater_indicator[:-1]
        * seawater_indicator[1:]
        * (MIXING_BASE + MIXING_CONV * jax.nn.sigmoid(-density_jump / DENSITY_SCALE))
    )
    ratio_prev = jnp.zeros(star.shape[2:], jnp.float32)
    value_prev = jnp.zeros(star[:, 0].shape, jnp.float32)
    ratios = []
    values = []
    for layer_index in range(layer_total):
        above = (
            mixing[layer_index - 1] if layer_index > 0 else jnp.zeros(star.shape[2:], jnp.float32)
        )
        below = (
            mixing[layer_index]
            if layer_index < layer_total - 1
            else jnp.zeros(star.shape[2:], jnp.float32)
        )
        pivot_value = 1.0 + above + below - above * ratio_prev
        value_prev = (star[:, layer_index] + above * value_prev) / pivot_value
        ratio_prev = below / pivot_value
        ratios.append(ratio_prev)
        values.append(value_prev)
    solved = [None] * layer_total
    solved[layer_total - 1] = values[layer_total - 1]
    for layer_index in range(layer_total - 2, -1, -1):
        solved[layer_index] = values[layer_index] + ratios[layer_index] * solved[layer_index + 1]
    return seawater_indicator * jnp.stack(solved, axis=1)


def local(
    potential_warmth,
    saltiness_psu,
    zonal_stability_ratio,
    poleward_stability_ratio,
    sinking_stability_ratio,
    seafloor_layer_index,
):
    layer_total, block_height_total, block_width_total = potential_warmth.shape
    level_ids = jnp.arange(layer_total, dtype=jnp.int32)[:, None, None]
    seawater_indicator = (level_ids < seafloor_layer_index[None]).astype(jnp.float32)

    def pack(stability_ratio):
        return jnp.concatenate(
            [potential_warmth, saltiness_psu, stability_ratio, seawater_indicator], axis=0
        )

    def unpack(packed):
        scalar_quantity = jnp.stack([packed[:layer_total], packed[layer_total : 2 * layer_total]])
        faces = packed[2 * layer_total : 3 * layer_total]
        wet_cells = packed[3 * layer_total :]
        return (scalar_quantity, faces, wet_cells)

    zonal = padded_2(pack(zonal_stability_ratio), (("ia", 2),), 2, True)
    merid_source = pack(poleward_stability_ratio)
    merid = padded_2(merid_source, (("ja", 1),), 2, False)
    mirrored = jnp.flip(merid_source[:, block_height_total - 2 :, :], axis=(1, 2))
    for bit_number in range(lax.axis_size("ia").bit_length() - 1):
        mirrored = partner(mirrored, "ia", bit_number)
    is_north = lax.axis_index("ja") == lax.axis_size("ja") - 1
    ghost_rows = jnp.where(is_north, mirrored, merid[:, block_height_total + 2 :, :])
    merid = jnp.concatenate([merid[:, : block_height_total + 2, :], ghost_rows], axis=1)
    merid_tracer, merid_courant, merid_wet = unpack(merid)
    zonal_tracer, zonal_courant, zonal_wet = unpack(zonal)
    north_faces = merid_courant[:, 1 : block_height_total + 2, :]
    mirrored_face = mirrored[2 * layer_total : 3 * layer_total, 0, :]
    last_face = jnp.where(is_north, 0.5 * (north_faces[:, -1] - mirrored_face), north_faces[:, -1])
    north_faces = jnp.concatenate([north_faces[:, :-1], last_face[:, None]], axis=1)
    east_faces = zonal_courant[:, :, 1 : block_width_total + 2]
    horizontal_part = tvd_divergence(zonal_tracer, zonal_wet, east_faces, -1) + tvd_divergence(
        merid_tracer, merid_wet, north_faces, -2
    )
    step_output = column_mixing_physics(
        jnp.stack([potential_warmth, saltiness_psu]),
        horizontal_part,
        sinking_stability_ratio,
        seawater_indicator,
    )
    return (step_output[0], step_output[1])


def solution(mesh):
    placed = (
        P(None, "ja", "ia"),
        P(None, "ja", "ia"),
        P(None, "ja", "ia"),
        P(None, "ja", "ia"),
        P(None, "ja", "ia"),
        P("ja", "ia"),
    )
    return jax.shard_map(
        local,
        mesh=mesh,
        in_specs=placed,
        out_specs=(P(None, "ja", "ia"), P(None, "ja", "ia")),
        check_vma=False,
    )
```

profile of v0, /device:TPU:14, one launch (start us, length us, event | category | flops | bytes accessed | tf_op | source)
XLA Modules:
  0.0 101.4 jit_solution(16909451260765288631)
XLA Ops:
  0.6 0.8 fusion.33
  1.4 3.2 %pad_maximum_fusion.2 = (f32[64,64,128]{2,1,0:T(8,128)S(1)}, f32[64,64,128]{2,1,0:T(8,128)}) fusion(f32[16,64,128]{2,1,0:T(8,128)S(1)} %fusion.33, f32[16,64,128]{2,1,0:T(8,128)} %param.8, f32[16,64,128]{2,1,0:T(8,128)} %param.7, f32[16,64,128]{2,1,0:T(8,128)} %param.6, f32[16,64,128]{2,1,0:T(8,128)} %param.9), kind=kLoop, calls=%fused_computation.8 | loop fusion | flops 2621440 | bytes 6815744 | tf_op jit(solution)/shard_map/concatenate | solution.py:140
  4.7 2.1 %fusion.85 = (f32[64,64,2]{2,1,0:T(8,128)}, f32[64,64,2]{2,1,0:T(8,128)S(1)}) fusion(f32[64,64,128]{2,1,0:T(8,128)S(1)} %get-tuple-element.53), kind=kLoop, calls=%fused_computation.234 | loop fusion | bytes 131072 | tf_op jit(solution)/shard_map/slice | solution.py:24
  6.8 2.3 %copy.47 = f32[64,64,2]{1,0,2:T(8,128)S(1)} copy(f32[64,64,2]{2,1,0:T(8,128)} %get-tuple-element.49) | data formatting | bytes 65536 | tf_op jit(solution)/shard_map/slice | solution.py:24
  9.0 3.8 %collective-permute-start = (f32[64,64,2]{1,0,2:T(8,128)S(1)}, f32[64,64,2]{1,0,2:T(8,128)S(1)}, u32[]{:S(2)}, u32[]{:S(2)}) collective-permute-start(f32[64,64,2]{1,0,2:T(8,128)S(1)} %copy.47), channel_id=1, source_target_pairs={{0,1},{1,2},{2,3},{3,4},{4,5},{5,6},{6,7},{7,8},{8,9},{9,10},{10,1... | collective-permute-start | bytes 98312 | tf_op jit(solution)/shard_map/ppermute | solution.py:27
  12.9 0.7 copy.49
  13.6 2.1 %collective-permute-start.1 = (f32[64,64,2]{1,0,2:T(8,128)S(1)}, f32[64,64,2]{1,0,2:T(8,128)S(1)}, u32[]{:S(2)}, u32[]{:S(2)}) collective-permute-start(f32[64,64,2]{1,0,2:T(8,128)S(1)} %copy.49), channel_id=1, source_target_pairs={{1,0},{2,1},{3,2},{4,3},{5,4},{6,5},{7,6},{8,7},{9,8},{10,9},{11,1... | collective-permute-start | bytes 98312 | tf_op jit(solution)/shard_map/ppermute | solution.py:29
  15.7 1.1 %fusion.86 = (f32[64,2,128]{2,1,0:T(2,128)S(1)}, f32[64,2,128]{2,1,0:T(2,128)S(1)}) fusion(f32[64,64,128]{2,1,0:T(8,128)} %get-tuple-element.54), kind=kLoop, calls=%fused_computation.235 | loop fusion | bytes 262144 | tf_op jit(solution)/shard_map/slice | solution.py:24
  16.8 0.3 rev.4
  17.1 0.6 copy.55
  17.7 10.8 %collective-permute-start.3 = (f32[64,2,128]{2,0,1:T(8,128)}, f32[64,2,128]{2,0,1:T(8,128)}, u32[]{:S(2)}, u32[]{:S(2)}) collective-permute-start(f32[64,2,128]{2,0,1:T(8,128)} %copy.55), channel_id=1, source_target_pairs={{0,1},{1,0},{2,3},{3,2},{4,5},{5,4},{6,7},{7,6},{8,9},{9,8},{10,11... | collective-permute-start | bytes 196616 | tf_op jit(solution)/shard_map/ppermute | solution.py:37
  28.6 0.6 copy.57
  29.2 1.9 %collective-permute-start.8 = (f32[64,2,128]{2,0,1:T(8,128)}, f32[64,2,128]{2,0,1:T(8,128)S(1)}, u32[]{:S(2)}, u32[]{:S(2)}) collective-permute-start(f32[64,2,128]{2,0,1:T(8,128)} %copy.57), channel_id=1, source_target_pairs={{32,0},{64,32},{96,64},{128,96},{160,128},{192,160},{224,192},{256... | collective-permute-start | bytes 196616 | tf_op jit(solution)/shard_map/ppermute | solution.py:29
  31.1 0.6 copy.52
  31.8 2.4 %collective-permute-start.2 = (f32[64,2,128]{2,0,1:T(8,128)}, f32[64,2,128]{2,0,1:T(8,128)}, u32[]{:S(2)}, u32[]{:S(2)}) collective-permute-start(f32[64,2,128]{2,0,1:T(8,128)} %copy.52), channel_id=1, source_target_pairs={{0,32},{32,64},{64,96},{96,128},{128,160},{160,192},{192,224},{224... | collective-permute-start | bytes 196616 | tf_op jit(solution)/shard_map/ppermute | solution.py:27
  34.2 0.1 fusion.29
  34.2 0.0 copy-start
  34.3 0.0 copy-start.1
  34.3 0.1 pad_compare_fusion
  34.4 0.1 slice_multiply_fusion.4
  34.5 0.8 copy-done
  35.3 0.2 copy-done.1
  35.4 0.1 pad_maximum_fusion.11
  35.6 0.2 fusion.11
  35.7 0.0 copy-start.3
  35.8 0.8 fusion.23
  36.6 0.2 copy-done.3
  36.8 0.0 collective-permute-done
  36.8 2.1 %copy.48 = f32[64,64,2]{2,1,0:T(8,128)} copy(f32[64,64,2]{1,0,2:T(8,128)S(1)} %collective-permute-done) | data formatting | bytes 65536 | tf_op jit(solution)/shard_map/ppermute | solution.py:27
  38.9 2.0 %copy.51 = f32[64,64,2]{2,1,0:T(8,128)} copy(f32[64,64,2]{1,0,2:T(8,128)S(1)} %collective-permute-done.1) | data formatting | bytes 65536 | tf_op jit(solution)/shard_map/ppermute | solution.py:29
  40.9 5.9 %pad_maximum_fusion = f32[64,64,132]{2,1,0:T(8,128)S(1)} fusion(f32[64,64,2]{2,1,0:T(8,128)} %copy.51, f32[16,64,128]{2,1,0:T(8,128)S(1)} %fusion.33, f32[16,64,128]{2,1,0:T(8,128)} %param.8, f32[16,64,128]{2,1,0:T(8,128)S(1)} %copy-done, f32[16,64,128]{2,1,0:T(8,128)S(1)} %copy-done.1, f32[64,64,2]{2,1,0:T(8,128)} %copy.48), kind=kLoop, calls=%fused_computation | loop fusion | flops 2703360 | bytes 4325376 | tf_op jit(solution)/shard_map/concatenate | solution.py:25
  46.8 0.0 copy-start.4
  46.8 0.3 slice_multiply_fusion.1
  47.2 1.2 %copy-done.2 = f32[64,64,2]{2,1,0:T(8,128)S(1)} copy-done((f32[64,64,2]{2,1,0:T(8,128)S(1)}, f32[64,64,2]{2,1,0:T(8,128)}, u32[]{:S(2)}) %copy-start.2) | copy-done | bytes 32792
  48.4 0.1 copy-done.4
  48.5 0.5 broadcast_compare_fusion
  49.0 1.9 %collective-permute-start.4 = (f32[64,2,128]{2,0,1:T(8,128)}, f32[64,2,128]{2,0,1:T(8,128)S(1)}, u32[]{:S(2)}, u32[]{:S(2)}) collective-permute-start(f32[64,2,128]{2,0,1:T(8,128)} %collective-permute-done.3), channel_id=1, source_target_pairs={{0,2},{1,3},{2,0},{3,1},{4,6},{5,7},{6,4},{7,5},{8,10},{9,11},{10,... | collective-permute-start | bytes 196616 | tf_op jit(solution)/shard_map/ppermute | solution.py:37
  50.9 0.4 slice_multiply_fusion
  51.3 4.1 %collective-permute-done.4 = f32[64,2,128]{2,0,1:T(8,128)S(1)} collective-permute-done((f32[64,2,128]{2,0,1:T(8,128)}, f32[64,2,128]{2,0,1:T(8,128)S(1)}, u32[]{:S(2)}, u32[]{:S(2)}) %collective-permute-start.4) | collective-permute-done | bytes 65568 | tf_op jit(solution)/shard_map/ppermute | solution.py:37
  55.3 1.9 %collective-permute-start.5 = (f32[64,2,128]{2,0,1:T(8,128)S(1)}, f32[64,2,128]{2,0,1:T(8,128)S(1)}, u32[]{:S(2)}, u32[]{:S(2)}) collective-permute-start(f32[64,2,128]{2,0,1:T(8,128)S(1)} %collective-permute-done.4), channel_id=1, source_target_pairs={{0,4},{1,5},{2,6},{3,7},{4,0},{5,1},{6,2},{7,3},{8,12},{9,13},{10,... | collective-permute-start | bytes 196616 | tf_op jit(solution)/shard_map/ppermute | solution.py:37
  57.3 0.1 slice_bitcast_fusion
  57.4 5.1 %collective-permute-done.5 = f32[64,2,128]{2,0,1:T(8,128)S(1)} collective-permute-done((f32[64,2,128]{2,0,1:T(8,128)S(1)}, f32[64,2,128]{2,0,1:T(8,128)S(1)}, u32[]{:S(2)}, u32[]{:S(2)}) %collective-permute-start.5) | collective-permute-done | bytes 65568 | tf_op jit(solution)/shard_map/ppermute | solution.py:37
  62.5 3.3 %collective-permute-start.6 = (f32[64,2,128]{2,0,1:T(8,128)S(1)}, f32[64,2,128]{2,0,1:T(8,128)S(1)}, u32[]{:S(2)}, u32[]{:S(2)}) collective-permute-start(f32[64,2,128]{2,0,1:T(8,128)S(1)} %collective-permute-done.5), channel_id=1, source_target_pairs={{0,8},{1,9},{2,10},{3,11},{4,12},{5,13},{6,14},{7,15},{8,0},{9,1},... | collective-permute-start | bytes 196616 | tf_op jit(solution)/shard_map/ppermute | solution.py:37
  65.8 0.7 fusion.2
  66.5 9.7 %collective-permute-done.6 = f32[64,2,128]{2,0,1:T(8,128)S(1)} collective-permute-done((f32[64,2,128]{2,0,1:T(8,128)S(1)}, f32[64,2,128]{2,0,1:T(8,128)S(1)}, u32[]{:S(2)}, u32[]{:S(2)}) %collective-permute-start.6) | collective-permute-done | bytes 65568 | tf_op jit(solution)/shard_map/ppermute | solution.py:37
  76.2 10.1 %collective-permute-start.7 = (f32[64,2,128]{2,0,1:T(8,128)S(1)}, f32[64,2,128]{2,0,1:T(8,128)S(1)}, u32[]{:S(2)}, u32[]{:S(2)}) collective-permute-start(f32[64,2,128]{2,0,1:T(8,128)S(1)} %collective-permute-done.6), channel_id=1, source_target_pairs={{0,16},{1,17},{2,18},{3,19},{4,20},{5,21},{6,22},{7,23},{8,24},{9,... | collective-permute-start | bytes 196616 | tf_op jit(solution)/shard_map/ppermute | solution.py:37
  86.2 3.2 %fusion.6 = f32[2,16,64,129]{3,2,1,0:T(8,128)S(1)} fusion(f32[1,16,64,132]{3,2,1,0:T(8,128)S(1)} %get-tuple-element.46, f32[1,16,64,132]{3,2,1,0:T(8,128)S(1)} %get-tuple-element.45, f32[2,16,64,131]{3,2,1,0:T(8,128)S(1)} %fusion.2, f32[16,64,129]{2,1,0:T(8,128)S(1)} %get-tuple-element.58, f32[16,64,129]{2,1,0:T(8,128)S(1)} %get-tuple-element.57, ...), kind=kLoop, calls=%fused_computation.16 | loop fusion | flops 5812224 | bytes 6497280 | tf_op jit(solution)/shard_map/mul | solution.py:73
  89.5 0.9 copy.53
  90.4 4.8 %collective-permute-done.7 = f32[64,2,128]{2,0,1:T(8,128)S(1)} collective-permute-done((f32[64,2,128]{2,0,1:T(8,128)S(1)}, f32[64,2,128]{2,0,1:T(8,128)S(1)}, u32[]{:S(2)}, u32[]{:S(2)}) %collective-permute-start.7) | collective-permute-done | bytes 65568 | tf_op jit(solution)/shard_map/ppermute | solution.py:37
  95.2 0.1 copy_select_fusion
  95.3 0.4 pad_maximum_fusion.3
  95.7 0.1 slice_bitcast_fusion.2
  95.8 0.1 slice_multiply_fusion.3
  95.8 0.1 broadcast_compare_fusion.1
  96.0 0.1 slice_multiply_fusion.2
  96.1 0.2 fusion.14
  96.3 1.8 %fusion.18 = f32[2,16,65,128]{3,2,1,0:T(8,128)S(1)} fusion(f32[1,16,68,128]{3,2,1,0:T(8,128)S(1)} %get-tuple-element.48, f32[1,16,68,128]{3,2,1,0:T(8,128)S(1)} %get-tuple-element.47, f32[2,16,67,128]{3,2,1,0:T(8,128)S(1)} %fusion.14, f32[16,65,128]{2,1,0:T(8,128)S(1)} %get-tuple-element.60, f32[16,65,128]{2,1,0:T(8,128)S(1)} %get-tuple-element.59, ...), kind=kLoop, calls=%fused_computation.40 | loop fusion | flops 5857280 | bytes 6572032 | tf_op jit(solution)/shard_map/mul | solution.py:73
  98.1 0.7 fusion.26
  98.8 0.3 multiply_subtract_fusion
  99.1 0.2 fusion.40
  99.5 0.1 subtract_bitcast_fusion
  99.6 0.3 add_dynamic-update-slice_fusion
  100.2 0.1 broadcast_multiply_fusion
  100.3 1.0 %slice_bitcast_fusion.4 = (f32[16,64,128]{2,1,0:T(8,128)}, f32[16,64,128]{2,1,0:T(8,128)}) fusion(f32[2,16,64,128]{3,2,1,0:T(8,128)S(1)} %broadcast_multiply_fusion), kind=kLoop, calls=%fused_computation.82 | loop fusion | bytes 2097152 | tf_op jit(solution)/shard_map/squeeze | solution.py:175
  (33 shorter events, 0.5 us)
Async XLA Ops:
  9.0 25.2 %copy-start.5 = (f32[16,64,128]{2,1,0:T(8,128)S(1)}, f32[16,64,128]{2,1,0:T(8,128)}, u32[]{:S(2)}) copy-start(f32[16,64,128]{2,1,0:T(8,128)} %param.10) | copy-start | bytes 1572868
  9.0 27.8 %collective-permute-start = (f32[64,64,2]{1,0,2:T(8,128)S(1)}, f32[64,64,2]{1,0,2:T(8,128)S(1)}, u32[]{:S(2)}, u32[]{:S(2)}) collective-permute-start(f32[64,64,2]{1,0,2:T(8,128)S(1)} %copy.47), channel_id=1, source_target_pairs={{0,1},{1,2},{2,3},{3,4},{4,5},{5,6},{6,7},{7,8},{8,9},{9,10},{10,1... | collective-permute-start | bytes 98312 | tf_op jit(solution)/shard_map/ppermute | solution.py:27
  13.6 25.3 %collective-permute-start.1 = (f32[64,64,2]{1,0,2:T(8,128)S(1)}, f32[64,64,2]{1,0,2:T(8,128)S(1)}, u32[]{:S(2)}, u32[]{:S(2)}) collective-permute-start(f32[64,64,2]{1,0,2:T(8,128)S(1)} %copy.49), channel_id=1, source_target_pairs={{1,0},{2,1},{3,2},{4,3},{5,4},{6,5},{7,6},{8,7},{9,8},{10,9},{11,1... | collective-permute-start | bytes 98312 | tf_op jit(solution)/shard_map/ppermute | solution.py:29
  17.7 31.2 %collective-permute-start.3 = (f32[64,2,128]{2,0,1:T(8,128)}, f32[64,2,128]{2,0,1:T(8,128)}, u32[]{:S(2)}, u32[]{:S(2)}) collective-permute-start(f32[64,2,128]{2,0,1:T(8,128)} %copy.55), channel_id=1, source_target_pairs={{0,1},{1,0},{2,3},{3,2},{4,5},{5,4},{6,7},{7,6},{8,9},{9,8},{10,11... | collective-permute-start | bytes 196616 | tf_op jit(solution)/shard_map/ppermute | solution.py:37
  29.2 61.1 %collective-permute-start.8 = (f32[64,2,128]{2,0,1:T(8,128)}, f32[64,2,128]{2,0,1:T(8,128)S(1)}, u32[]{:S(2)}, u32[]{:S(2)}) collective-permute-start(f32[64,2,128]{2,0,1:T(8,128)} %copy.57), channel_id=1, source_target_pairs={{32,0},{64,32},{96,64},{128,96},{160,128},{192,160},{224,192},{256... | collective-permute-start | bytes 196616 | tf_op jit(solution)/shard_map/ppermute | solution.py:29
  31.8 57.7 %collective-permute-start.2 = (f32[64,2,128]{2,0,1:T(8,128)}, f32[64,2,128]{2,0,1:T(8,128)}, u32[]{:S(2)}, u32[]{:S(2)}) collective-permute-start(f32[64,2,128]{2,0,1:T(8,128)} %copy.52), channel_id=1, source_target_pairs={{0,32},{32,64},{64,96},{96,128},{128,160},{160,192},{192,224},{224... | collective-permute-start | bytes 196616 | tf_op jit(solution)/shard_map/ppermute | solution.py:27
  34.2 1.0 %copy-start = (f32[16,64,128]{2,1,0:T(8,128)S(1)}, f32[16,64,128]{2,1,0:T(8,128)}, u32[]{:S(2)}) copy-start(f32[16,64,128]{2,1,0:T(8,128)} %param.7) | copy-start | bytes 1572868
  34.3 1.2 %copy-start.1 = (f32[16,64,128]{2,1,0:T(8,128)S(1)}, f32[16,64,128]{2,1,0:T(8,128)}, u32[]{:S(2)}) copy-start(f32[16,64,128]{2,1,0:T(8,128)} %param.6) | copy-start | bytes 1572868
  35.7 1.0 %copy-start.3 = (f32[16,64,128]{2,1,0:T(8,128)S(1)}, f32[16,64,128]{2,1,0:T(8,128)}, u32[]{:S(2)}) copy-start(f32[16,64,128]{2,1,0:T(8,128)} %param.9) | copy-start | bytes 1572868
  46.8 1.6 %copy-start.2 = (f32[64,64,2]{2,1,0:T(8,128)S(1)}, f32[64,64,2]{2,1,0:T(8,128)}, u32[]{:S(2)}) copy-start(f32[64,64,2]{2,1,0:T(8,128)} %copy.48) | copy-start | bytes 98308
  46.8 1.7 %copy-start.4 = (f32[16,64,128]{2,1,0:T(8,128)S(1)}, f32[16,64,128]{2,1,0:T(8,128)}, u32[]{:S(2)}) copy-start(f32[16,64,128]{2,1,0:T(8,128)} %param.8) | copy-start | bytes 1572868
  49.0 6.4 %collective-permute-start.4 = (f32[64,2,128]{2,0,1:T(8,128)}, f32[64,2,128]{2,0,1:T(8,128)S(1)}, u32[]{:S(2)}, u32[]{:S(2)}) collective-permute-start(f32[64,2,128]{2,0,1:T(8,128)} %collective-permute-done.3), channel_id=1, source_target_pairs={{0,2},{1,3},{2,0},{3,1},{4,6},{5,7},{6,4},{7,5},{8,10},{9,11},{10,... | collective-permute-start | bytes 196616 | tf_op jit(solution)/shard_map/ppermute | solution.py:37
  55.3 7.2 %collective-permute-start.5 = (f32[64,2,128]{2,0,1:T(8,128)S(1)}, f32[64,2,128]{2,0,1:T(8,128)S(1)}, u32[]{:S(2)}, u32[]{:S(2)}) collective-permute-start(f32[64,2,128]{2,0,1:T(8,128)S(1)} %collective-permute-done.4), channel_id=1, source_target_pairs={{0,4},{1,5},{2,6},{3,7},{4,0},{5,1},{6,2},{7,3},{8,12},{9,13},{10,... | collective-permute-start | bytes 196616 | tf_op jit(solution)/shard_map/ppermute | solution.py:37
  62.5 13.6 %collective-permute-start.6 = (f32[64,2,128]{2,0,1:T(8,128)S(1)}, f32[64,2,128]{2,0,1:T(8,128)S(1)}, u32[]{:S(2)}, u32[]{:S(2)}) collective-permute-start(f32[64,2,128]{2,0,1:T(8,128)S(1)} %collective-permute-done.5), channel_id=1, source_target_pairs={{0,8},{1,9},{2,10},{3,11},{4,12},{5,13},{6,14},{7,15},{8,0},{9,1},... | collective-permute-start | bytes 196616 | tf_op jit(solution)/shard_map/ppermute | solution.py:37
  76.2 19.1 %collective-permute-start.7 = (f32[64,2,128]{2,0,1:T(8,128)S(1)}, f32[64,2,128]{2,0,1:T(8,128)S(1)}, u32[]{:S(2)}, u32[]{:S(2)}) collective-permute-start(f32[64,2,128]{2,0,1:T(8,128)S(1)} %collective-permute-done.6), channel_id=1, source_target_pairs={{0,16},{1,17},{2,18},{3,19},{4,20},{5,21},{6,22},{7,23},{8,24},{9,... | collective-permute-start | bytes 196616 | tf_op jit(solution)/shard_map/ppermute | solution.py:37
where the time goes:
time: 102 us; the launch traced here: 101 us
  starting transfers between devices  38.3 us (38%)
  waiting for transfers between devices  23.7 us (23%)
  other arithmetic  21 us (21%)
  local copies, waits for them, and re-layouts  17.1 us (17%)
  between operations  1.17 us (1%)
    ppermute x5, starting transfers between devices, partner(): lax.ppermute(x, axis, [(i, i ^ 1 << apart) for i in range(lax.axis_size(a...  28 us
    ppermute x5, waiting for transfers between devices, partner(): lax.ppermute(x, axis, [(i, i ^ 1 << apart) for i in range(lax.axis_size(a...  23.7 us
    mul x6, other arithmetic, tvd_divergence(): flux = stability_ratio * open_face * face_value  6.44 us
    ppermute x2, starting transfers between devices, padded_2(): lax.ppermute(tail, axis, [(i, (i + 1) % count) for i in range(ends)])  6.24 us
    slice x4, local copies, waits for them, and re-layouts, padded_2(): lax.slice_in_dim(cells, cells.shape[dim] - width, cells.shape[dim], axis=...  6.05 us
    concatenate x1, other arithmetic, padded_2(): jnp.concatenate([lax.ppermute(tail, axis, [(i, (i + 1) % count) for i in...  5.86 us
    ppermute x2, starting transfers between devices, padded_2(): lax.ppermute(head, axis, [((i + 1) % count, i) for i in range(ends)])  4.04 us
    concatenate x1, other arithmetic, pack(): jnp.concatenate([potential_warmth, saltiness_psu, stability_ratio, seawat...  3.25 us
  transfers between devices with their start and end apart: 9, of which 4 were waited for; matrix products, arithmetic and copies ran while one was open for 21% of the time, Pallas kernels for 0%

commit v1 on v0

v1 whole, which is shorter than its diff:
```python
import functools

import jax
import jax.numpy as jnp
from jax import lax
from jax.experimental import pallas as pl
from jax.experimental.pallas import tpu as pltpu
from jax.sharding import PartitionSpec as P

THERMAL_COEF = 0.1655
HALINE_COEF = 0.76554
CABBELING_T = 0.05952
CABBELING_S = 0.00054914
THERMOBARIC_T = 0.0001497
THERMOBARIC_S = 1.109e-05
MIXED_COEF = 0.0024341
LAYER_DEPTH = 50.0

NK = 16
NJ = 64
NI = 128
NB = NJ // 8
F32 = jnp.float32

COLS = (-3, -2, -1, 0, 1, 2)
ROWS = (0, 1, 2, 61, 62, 63)
MROWS = 88


def lanes():
    return lax.broadcasted_iota(jnp.int32, (8, NI), 1)


def sublanes():
    return lax.broadcasted_iota(jnp.int32, (8, NI), 0)


def minmod(x, y):
    return jnp.maximum(jnp.minimum(x, jnp.maximum(y, 0.0)), jnp.minimum(y, 0.0))


def slope_factor(c):
    return jnp.where(c > 0, 0.5, -0.5) - 0.5 * c


def flux(c, c_open, factor, qa, sa, qb, sb):
    up = c > 0
    return c_open * (jnp.where(up, qa, qb) + factor * jnp.where(up, sa, sb))


def pack_kernel(
    t_hbm, s_hbm, u_hbm, v_hbm, w_hbm, k_hbm, east_ref, west_ref, p1_ref, p2_ref, own_ref,
    t_ref, s_ref, u_ref, v_ref, w_ref, k_ref, sems,
):
    chunks = 4
    per = NK // chunks
    copies = []
    for c in range(chunks):
        part = pl.ds(c * per, per)
        for f, (src, dst) in enumerate(((t_hbm, t_ref), (s_hbm, s_ref), (u_hbm, u_ref))):
            copies.append(pltpu.make_async_copy(src.at[part], dst.at[part], sems.at[c * 3 + f]))
    late = [
        pltpu.make_async_copy(k_hbm, k_ref, sems.at[12]),
        pltpu.make_async_copy(v_hbm, v_ref, sems.at[13]),
        pltpu.make_async_copy(w_hbm, w_ref, sems.at[14]),
    ]
    for c in copies + late:
        c.start()

    lane = lanes()
    even = lax.rem(lax.axis_index("ja"), 2) == 0
    near1 = jnp.where(even, NJ - 1, 0)
    far1 = jnp.where(even, NJ - 2, 1)
    near2 = jnp.where(even, 0, NJ - 1)
    far2 = jnp.where(even, 1, NJ - 2)
    rows = ((p1_ref, near1, far1), (p2_ref, near2, far2))

    def windows(blocks, k, window):
        out = pltpu.roll(blocks[0], k, 1)
        for b in range(1, NB):
            out = jnp.where(window == b, pltpu.roll(blocks[b], b * 16 + k, 1), out)
        return out

    t_acc = [None] * 6
    s_acc = [None] * 6
    u_acc = [None] * 6
    for k in range(NK):
        if k % per == 0:
            for c in copies[k // per * 3 : k // per * 3 + 3]:
                c.wait()
        place = (lane - (k - 3)) & (NI - 1)
        window = lax.shift_right_logical(place, 4)
        within = place & 15
        for ref, acc, which in ((t_ref, t_acc, range(6)), (s_ref, s_acc, range(6)), (u_ref, u_acc, (1, 2, 3))):
            got = windows([ref[k, pl.ds(8 * b, 8), :] for b in range(NB)], k, window)
            for n in which:
                acc[n] = got if k == 0 else jnp.where(within == n, got, acc[n])
        for ref, near, far in rows:
            ref[pl.ds(k, 1), :] = t_ref[k, pl.ds(near, 1), :]
            ref[pl.ds(16 + k, 1), :] = t_ref[k, pl.ds(far, 1), :]
            ref[pl.ds(32 + k, 1), :] = s_ref[k, pl.ds(near, 1), :]
            ref[pl.ds(48 + k, 1), :] = s_ref[k, pl.ds(far, 1), :]
    for c in late:
        c.wait()
    for ref, near, far in rows:
        for k in range(NK):
            ref[pl.ds(64 + k, 1), :] = v_ref[k, pl.ds(near, 1), :]
        ref[pl.ds(80, 8), :] = jnp.zeros((8, NI), F32)
        ref[pl.ds(80, 1), :] = k_ref[pl.ds(near, 1), :].astype(F32)
        ref[pl.ds(81, 1), :] = k_ref[pl.ds(far, 1), :].astype(F32)

    place = (lane + 3) & (NI - 1)
    floor = windows([k_ref[pl.ds(8 * b, 8), :].astype(F32) for b in range(NB)], 0, lax.shift_right_logical(place, 4))
    first = (lane & 15) == 0
    k_cols = []
    for n, off in enumerate(COLS):
        x = jnp.where(first, pltpu.roll(floor, -off % NI, 1), 0.0)
        for step in (1, 2, 4, 8):
            x = x + pltpu.roll(x, step, 1)
        k_cols.append(x)
    t_cols = [pltpu.roll(x, -off % NI, 1) for x, off in zip(t_acc, COLS)]
    s_cols = [pltpu.roll(x, -off % NI, 1) for x, off in zip(s_acc, COLS)]
    u_cols = [pltpu.roll(u_acc[n], -COLS[n] % NI, 1) for n in (1, 2, 3)]
    for n, x in enumerate(t_cols + s_cols + k_cols + u_cols):
        own_ref[n] = x
    for n, x in enumerate((t_cols[2], t_cols[1], s_cols[2], s_cols[1], k_cols[2], k_cols[1], u_cols[1])):
        east_ref[n] = x
    for n, x in enumerate((t_cols[3], t_cols[4], s_cols[3], s_cols[4], k_cols[3], k_cols[4])):
        west_ref[n] = x


def pack(t, s, u, v, w, floor):
    fields = [pltpu.with_memory_space_constraint(x, pltpu.HBM) for x in (t, s, u, v, w, floor)]
    return pl.pallas_call(
        pack_kernel,
        out_shape=tuple(
            pltpu.VMEM(shape, F32) for shape in ((7, 8, NI), (6, 8, NI), (MROWS, NI), (MROWS, NI), (21, 8, NI))
        )
        + (pltpu.VMEM((NK, NJ, NI), F32),) * 5
        + (pltpu.VMEM((NJ, NI), jnp.int32),),
        in_specs=[pl.BlockSpec(memory_space=pltpu.HBM)] * 6,
        out_specs=(pl.BlockSpec(memory_space=pltpu.VMEM),) * 11,
        scratch_shapes=[pltpu.SemaphoreType.DMA((15,))],
        compiler_params=pltpu.CompilerParams(vmem_limit_bytes=16 * 2**20),
        name="pack_edges",
    )(*fields)


def bulk_kernel(t_ref, s_ref, u_ref, v_ref, w_ref, k_ref, to_ref, so_ref, rows_ref, th_ref, sh_ref, mask_ref):
    lane = lanes()
    sub = sublanes()
    floors = [k_ref[pl.ds(m, 8, stride=8), :] for m in range(NB)]
    for m in range(NB):
        east = jnp.where(lane == NI - 1, 0, jnp.minimum(floors[m], pltpu.roll(floors[m], NI - 1, 1)))
        if m < NB - 1:
            north = jnp.minimum(floors[m], floors[m + 1])
        else:
            north = jnp.where(sub == 7, 0, jnp.minimum(floors[m], pltpu.roll(floors[0], 7, 0)))
        mask_ref[0, m] = east
        mask_ref[1, m] = jnp.where((lane == 0) | (lane == NI - 2), 0, east)
        mask_ref[2, m] = north
        inner = north
        if m == 0:
            inner = jnp.where(sub == 0, 0, inner)
        if m == NB - 2:
            inner = jnp.where(sub == 7, 0, inner)
        mask_ref[3, m] = inner

    def level(k):
        q = [[ref[k, pl.ds(m, 8, stride=8), :] for m in range(NB)] for ref in (t_ref, s_ref)]
        c = [v_ref[k, pl.ds(m, 8, stride=8), :] for m in range(NB)]
        c_open = [jnp.where(mask_ref[3, m] > k, c[m], 0.0) for m in range(NB)]
        is_open = [mask_ref[2, m] > k for m in range(NB)]
        factor = [slope_factor(x) for x in c]
        left = []
        for x in q:
            after = x[1:] + [pltpu.roll(x[0], 7, 0)]
            g = [jnp.where(o, b - a, 0.0) for o, a, b in zip(is_open, x, after)]
            g_before = [pltpu.roll(g[-1], 1, 0)] + g[:-1]
            slope = [minmod(a, b) for a, b in zip(g, g_before)]
            slope_after = slope[1:] + [pltpu.roll(slope[0], 7, 0)]
            f = [flux(*y) for y in zip(c, c_open, factor, x, slope, after, slope_after)]
            f_before = [pltpu.roll(f[-1], 1, 0)] + f[:-1]
            left.append([a - (b - d) for a, b, d in zip(x, f, f_before)])
        for m in range(NB):
            c = u_ref[k, pl.ds(m, 8, stride=8), :]
            c_open = jnp.where(mask_ref[1, m] > k, c, 0.0)
            is_open = mask_ref[0, m] > k
            factor = slope_factor(c)
            for n, out in ((0, th_ref), (1, sh_ref)):
                x = q[n][m]
                after = pltpu.roll(x, NI - 1, 1)
                g = jnp.where(is_open, after - x, 0.0)
                slope = minmod(g, pltpu.roll(g, 1, 1))
                f = flux(c, c_open, factor, x, slope, after, pltpu.roll(slope, NI - 1, 1))
                out[k, pl.ds(m, 8, stride=8), :] = left[n][m] - (f - pltpu.roll(f, 1, 1))

    @pl.loop(0, NK, unroll=4)
    def _(k):
        level(k)

    def column(b, _):
        at = pl.ds(pl.multiple_of(b * 8, 8), 8)
        floor = k_ref[at, :]
        c = [w_ref[k, at, :] for k in range(NK - 1)]
        is_open = [floor > k + 1 for k in range(NK - 1)]
        c_open = [jnp.where(o, x, 0.0) for o, x in zip(is_open, c)]
        factor = [slope_factor(x) for x in c]
        for src, half, out in ((t_ref, th_ref, to_ref), (s_ref, sh_ref, so_ref)):
            x = [src[k, at, :] for k in range(NK)]
            g = [jnp.where(is_open[k], x[k + 1] - x[k], 0.0) for k in range(NK - 1)]
            slope = [jnp.zeros((8, NI), F32)] + [minmod(g[k], g[k - 1]) for k in range(1, NK - 1)] + [jnp.zeros((8, NI), F32)]
            before = None
            for k in range(NK):
                y = half[k, at, :]
                if k < NK - 1:
                    f = flux(c[k], c_open[k], factor[k], x[k], slope[k], x[k + 1], slope[k + 1])
                    y = y - (f if before is None else f - before)
                    before = f
                else:
                    y = y + before
                out[k, at, :] = y
        return 0

    lax.fori_loop(0, NB, column, 0)

    for n, r in enumerate(ROWS):
        for k in range(NK):
            rows_ref[n, pl.ds(k, 1), :] = t_ref[k, pl.ds(r, 1), :]
            rows_ref[6 + n, pl.ds(k, 1), :] = s_ref[k, pl.ds(r, 1), :]
    for n, r in enumerate((0, 62, 63)):
        for k in range(NK):
            rows_ref[12 + n, pl.ds(k, 1), :] = v_ref[k, pl.ds(r, 1), :]


def bulk(t, s, u, v, w, floor):
    vmem = pl.BlockSpec(memory_space=pltpu.VMEM)
    field = pltpu.VMEM((NK, NJ, NI), F32)
    return pl.pallas_call(
        bulk_kernel,
        out_shape=(
            pltpu.VMEM((NK, NJ, NI), F32),
            pltpu.VMEM((NK, NJ, NI), F32),
            pltpu.VMEM((15, NK, NI), F32),
        ),
        in_specs=[vmem] * 6,
        out_specs=(vmem,) * 3,
        scratch_shapes=[field, field, pltpu.VMEM((4, NB, 8, NI), jnp.int32)],
        compiler_params=pltpu.CompilerParams(vmem_limit_bytes=16 * 2**20),
        cost_estimate=pl.CostEstimate(flops=16_000_000, bytes_accessed=4_000_000, transcendentals=0),
        name="bulk_fluxes",
    )(t, s, u, v, w, floor)


def edge_fluxes(level, q, floor, c):
    is_open = [level < jnp.minimum(a, b) for a, b in zip(floor, floor[1:])]
    g = [jnp.where(o, b - a, 0.0) for o, a, b in zip(is_open, q, q[1:])]
    slope = [None] + [minmod(a, b) for a, b in zip(g, g[1:])]
    out = []
    for n, x in zip((1, 2), c):
        out.append(flux(x, jnp.where(is_open[n], x, 0.0), slope_factor(x), q[n], slope[n], q[n + 1], slope[n + 1]))
    return out


def solve_kernel(
    ts_ref, ss_ref, k_ref, own_ref, east_ref, west_ref, p1_ref, p2_ref, rows_ref, tn_hbm, sn_hbm,
    to_ref, so_ref, zonal_ref, merid_ref, out_sems,
):
    lane = lanes()
    ja = lax.axis_index("ja")
    even = lax.rem(ja, 2) == 0
    is_north = ja == lax.axis_size("ja") - 1

    level = (lane & 15).astype(F32)
    own = [own_ref[n] for n in range(21)]
    k_own = own[12:18]
    u_own = own[18:21]
    west_floor = [east_ref[5], east_ref[4]] + k_own[3:6]
    east_floor = k_own[0:3] + [west_ref[4], west_ref[5]]
    for n in range(2):
        q = own[6 * n : 6 * n + 6]
        f0, f1 = edge_fluxes(level, [east_ref[2 * n + 1], east_ref[2 * n]] + q[3:6], west_floor, (east_ref[6], u_own[2]))
        f2, f3 = edge_fluxes(level, q[0:3] + [west_ref[2 * n], west_ref[2 * n + 1]], east_floor, (u_own[0], u_own[1]))
        parts = (f2, f3 - f2, f1 - f0, -f1)
        for r in range(4):
            x = parts[0] if r == 0 else pltpu.roll(parts[0], (0 - r) % NI, 1)
            for i in range(1, 4):
                moved = parts[i] if i == r else pltpu.roll(parts[i], (i - r) % NI, 1)
                x = jnp.where((lane & 3) == i, moved, x)
            zonal_ref[n, r] = x

    level = lax.broadcasted_iota(jnp.int32, (NK, NI), 0).astype(F32)
    turned = NI - 1 - lanes()
    p1 = [p1_ref[pl.ds(8 * n, 8), :] for n in range(MROWS // 8)]
    p2 = [p2_ref[pl.ds(8 * n, 8), :] for n in range(MROWS // 8)]
    south = [jnp.where(even, b, a) for a, b in zip(p1, p2)]
    north = [jnp.where(is_north, jnp.take_along_axis(b, turned, axis=1), jnp.where(even, a, b)) for a, b in zip(p1, p2)]

    def plane(msg, n):
        return jnp.concatenate([msg[2 * n], msg[2 * n + 1]], axis=0)

    def wide(row):
        return jnp.broadcast_to(row, (NK, NI))

    floors = [wide(k_ref[pl.ds(r, 1), :].astype(F32)) for r in ROWS]
    s_floor = [wide(south[10][1:2]), wide(south[10][0:1])] + floors[0:3]
    n_floor = floors[3:6] + [wide(north[10][0:1]), wide(north[10][1:2])]
    last = jnp.where(is_north, 0.5 * (rows_ref[14] - plane(north, 4)), rows_ref[14])
    merid_ref[...] = jnp.zeros_like(merid_ref)
    for n in range(2):
        q = [rows_ref[6 * n + r] for r in range(6)]
        f0, f1 = edge_fluxes(level, [plane(south, 2 * n + 1), plane(south, 2 * n)] + q[0:3], s_floor, (plane(south, 4), rows_ref[12]))
        f2, f3 = edge_fluxes(level, q[3:6] + [plane(north, 2 * n), plane(north, 2 * n + 1)], n_floor, (rows_ref[13], last))
        for side, r, x in ((0, 0, f1 - f0), (0, 1, -f1), (2, 6, f2), (2, 7, f3 - f2)):
            for k in range(NK):
                merid_ref[n, side, k, pl.ds(r, 1), :] = x[k : k + 1]

    edge_lanes = (lane < 2) | (lane >= NI - 2)

    def column(b, _):
        at = pl.ds(pl.multiple_of(b * 8, 8), 8)
        side = jnp.where(b == 0, 0, jnp.where(b == NB - 1, 2, 1))
        floor = k_ref[at, :]
        wet = [floor > k for k in range(NK)]
        star = []
        for n, ref in enumerate((ts_ref, ss_ref)):
            star.append([])
            for k in range(NK):
                amount = lax.rem(2 * NI - 2 - 4 * (k // 4) - 16 * b, NI)
                z = pltpu.roll(zonal_ref[n, k % 4], amount, 1)
                x = ref[k, at, :] - (jnp.where(edge_lanes, z, 0.0) + merid_ref[n, side, k])
                star[n].append(jnp.where(wet[k], x, 0.0))
        dens = []
        for k in range(NK):
            z = LAYER_DEPTH * (k + 0.5)
            ta = star[0][k] - 10.0
            sa = star[1][k] - 35.0
            heat = (-0.5 * THERMAL_COEF * CABBELING_T) * ta - MIXED_COEF * sa - THERMAL_COEF * (1.0 + THERMOBARIC_T * z)
            salt = (-0.5 * HALINE_COEF * CABBELING_S) * sa + HALINE_COEF * (1.0 - THERMOBARIC_S * z)
            dens.append(heat * ta + salt * sa)
        above = None
        ratio = []
        values = ([], [])
        for k in range(NK):
            if k < NK - 1:
                below = jnp.where(wet[k + 1], 5.5 - 5.0 * jnp.tanh(dens[k + 1] - dens[k]), 0.0)
                pivot = 1.0 + below
            else:
                below = None
                pivot = 1.0
            if k > 0:
                pivot = pivot + above * (1.0 - ratio[-1])
            r = pl.reciprocal(pivot, approx=True)
            r = r * (2.0 - pivot * r)
            if below is not None:
                ratio.append(below * r)
            for n in range(2):
                x = star[n][k]
                if k > 0:
                    x = x + above * values[n][-1]
                values[n].append(x * r)
            above = below
        for n, out in enumerate((to_ref, so_ref)):
            x = values[n][NK - 1]
            out[NK - 1, at, :] = jnp.where(wet[NK - 1], x, 0.0)
            for k in range(NK - 2, -1, -1):
                x = values[n][k] + ratio[k] * x
                out[k, at, :] = jnp.where(wet[k], x, 0.0)
        pltpu.make_async_copy(to_ref.at[:, at], tn_hbm.at[:, at], out_sems.at[0, b]).start()
        pltpu.make_async_copy(so_ref.at[:, at], sn_hbm.at[:, at], out_sems.at[1, b]).start()
        return 0

    lax.fori_loop(0, NB, column, 0)
    for b in range(NB):
        at = pl.ds(b * 8, 8)
        pltpu.make_async_copy(to_ref.at[:, at], tn_hbm.at[:, at], out_sems.at[0, b]).wait()
        pltpu.make_async_copy(so_ref.at[:, at], sn_hbm.at[:, at], out_sems.at[1, b]).wait()


def solve(ts, ss, floor, own, east, west, p1, p2, rows):
    any_ = pl.BlockSpec(memory_space=pltpu.HBM)
    vmem = pl.BlockSpec(memory_space=pltpu.VMEM)
    field = pltpu.VMEM((NK, NJ, NI), F32)
    return pl.pallas_call(
        solve_kernel,
        out_shape=(jax.ShapeDtypeStruct((NK, NJ, NI), F32),) * 2,
        in_specs=[vmem] * 9,
        out_specs=(any_, any_),
        scratch_shapes=[field] * 2
        + [
            pltpu.VMEM((2, 4, 8, NI), F32),
            pltpu.VMEM((2, 3, NK, 8, NI), F32),
            pltpu.SemaphoreType.DMA((2, NB)),
        ],
        compiler_params=pltpu.CompilerParams(vmem_limit_bytes=16 * 2**20),
        cost_estimate=pl.CostEstimate(flops=6_000_000, bytes_accessed=2_500_000, transcendentals=300_000),
        name="solve_columns",
    )(ts, ss, floor, own, east, west, p1, p2, rows)


def local(nj, ni, t, s, u, v, w, floor):
    east, west, p1, p2, own, t, s, u, v, w, floor = pack(t, s, u, v, w, floor)
    east_pairs = [(i, (i + 1) % ni) for i in range(ni)]
    west_pairs = [((i + 1) % ni, i) for i in range(ni)]
    first = []
    second = []
    for i in range(ni):
        for j in range(0, nj, 2):
            first += [(j * ni + i, (j + 1) * ni + i), ((j + 1) * ni + i, j * ni + i)]
        for j in range(1, nj - 1, 2):
            second += [(j * ni + i, (j + 1) * ni + i), ((j + 1) * ni + i, j * ni + i)]
        second.append(((nj - 1) * ni + i, (nj - 1) * ni + ni - 1 - i))
    from_west = lax.ppermute(east, "ia", east_pairs)
    q1 = lax.ppermute(p1, ("ja", "ia"), first)
    q2 = lax.ppermute(p2, ("ja", "ia"), second)
    from_east = lax.ppermute(west, "ia", west_pairs)
    ts, ss, rows = bulk(t, s, u, v, w, floor)
    return solve(ts, ss, floor, own, from_west, from_east, q1, q2, rows)


def solution(mesh):
    field = P(None, "ja", "ia")
    return jax.shard_map(
        functools.partial(local, mesh.shape["ja"], mesh.shape["ia"]),
        mesh=mesh,
        in_specs=(field,) * 5 + (P("ja", "ia"),),
        out_specs=(field, field),
        check_vma=False,
    )
```

time: 102 us -> 32 us (0.31)
  the two profiles are of different devices: /device:TPU:14 before, /device:TPU:127 now
where the time goes in v1:
time: 32 us; the launch traced here: 31.8 us
  starting transfers between devices  20.3 us (63%)
  Pallas kernels  8.94 us (28%)
  waiting for transfers between devices  1.82 us (6%)
  between operations  0.68 us (2%)
    ppermute x1, starting transfers between devices, local(): q2 = lax.ppermute(p2, ('ja', 'ia'), second)  11.3 us
    ppermute x1, starting transfers between devices, local(): from_west = lax.ppermute(east, 'ia', east_pairs)  4.57 us
    pallas_call x1, Pallas kernels, solve(): pl.pallas_call(solve_kernel, out_shape=(jax.ShapeDtypeStruct((NK, NJ, NI)...  3.62 us
    pallas_call x1, Pallas kernels, bulk(): pl.pallas_call(bulk_kernel, out_shape=(pltpu.VMEM((NK, NJ, NI), F32), plt...  2.93 us
    ppermute x1, starting transfers between devices, local(): q1 = lax.ppermute(p1, ('ja', 'ia'), first)  2.59 us
    pallas_call x1, Pallas kernels, pack(): pl.pallas_call(pack_kernel, out_shape=tuple((pltpu.VMEM(shape, F32) for s...  2.39 us
    ppermute x1, starting transfers between devices, local(): from_east = lax.ppermute(west, 'ia', west_pairs)  1.92 us
    ppermute x1, waiting for transfers between devices, local(): from_east = lax.ppermute(west, 'ia', west_pairs)  1.81 us
  transfers between devices with their start and end apart: 4, of which 1 were waited for; matrix products, arithmetic and copies ran while one was open for 0% of the time, Pallas kernels for 9%

profile of v1, /device:TPU:127, one launch (start us, length us, event | category | flops | bytes accessed | tf_op | source)
XLA Modules:
  0.0 31.8 jit_solution(14845888060022005090)
XLA Ops:
  0.6 2.4 %pack_edges.1 = (f32[7,8,128]{2,1,0:T(8,128)S(1)}, f32[6,8,128]{2,1,0:T(8,128)S(1)}, f32[88,128]{1,0:T(8,128)S(1)}, f32[88,128]{1,0:T(8,128)S(1)}, f32[21,8,128]...) custom-call(f32[16,64,128]{2,1,0:T(8,128)} %t_hbm.1, ...), custom_call_target="tpu_custom_call" | custom-call | tf_op jit(solution)/shard_map/pack_edges/pallas_call | solution.py:134
  3.0 2.6 %collective-permute-start.2 = (f32[88,128]{1,0:T(8,128)S(1)}, f32[88,128]{1,0:T(8,128)S(1)}, u32[]{:S(2)}, u32[]{:S(2)}) collective-permute-start(f32[88,128]{1,0:T(8,128)S(1)} %get-tuple-element.27), channel_id=1, source_target_pairs={{0,32},{32,0},{64,96},{96,64},{128,160},{160,128},{192,224},{224,1... | collective-permute-start | bytes 135176 | tf_op jit(solution)/shard_map/ppermute | solution.py:414
  5.6 11.3 %collective-permute-start.3 = (f32[88,128]{1,0:T(8,128)S(1)}, f32[88,128]{1,0:T(8,128)S(1)}, u32[]{:S(2)}, u32[]{:S(2)}) collective-permute-start(f32[88,128]{1,0:T(8,128)S(1)} %get-tuple-element.28), channel_id=1, source_target_pairs={{32,64},{64,32},{96,128},{128,96},{160,192},{192,160},{224,256},{2... | collective-permute-start | bytes 135176 | tf_op jit(solution)/shard_map/ppermute | solution.py:415
  16.9 4.6 %collective-permute-start = (f32[7,8,128]{2,1,0:T(8,128)S(1)}, f32[7,8,128]{2,1,0:T(8,128)S(1)}, u32[]{:S(2)}, u32[]{:S(2)}) collective-permute-start(f32[7,8,128]{2,1,0:T(8,128)S(1)} %get-tuple-element.25), channel_id=1, source_target_pairs={{0,1},{1,2},{2,3},{3,4},{4,5},{5,6},{6,7},{7,8},{8,9},{9,10},{10,1... | collective-permute-start | bytes 86024 | tf_op jit(solution)/shard_map/ppermute | solution.py:413
  21.5 1.9 %collective-permute-start.1 = (f32[6,8,128]{2,1,0:T(8,128)S(1)}, f32[6,8,128]{2,1,0:T(8,128)S(1)}, u32[]{:S(2)}, u32[]{:S(2)}) collective-permute-start(f32[6,8,128]{2,1,0:T(8,128)S(1)} %get-tuple-element.26), channel_id=1, source_target_pairs={{1,0},{2,1},{3,2},{4,3},{5,4},{6,5},{7,6},{8,7},{9,8},{10,9},{11,1... | collective-permute-start | bytes 73736 | tf_op jit(solution)/shard_map/ppermute | solution.py:416
  23.4 2.9 %bulk_fluxes.1 = (f32[16,64,128]{2,1,0:T(8,128)S(1)}, f32[16,64,128]{2,1,0:T(8,128)S(1)}, f32[15,16,128]{2,1,0:T(8,128)S(1)}) custom-call(f32[16,64,128]{2,1,0:T(8,128)S(1)} %get-tuple-element.16.t_ref, f32[16,64,128]{2,1,0:T(8,128)S(1)} %get-tuple-element.17.s_ref, f32[16,64,128]{2,1,0:T(8,128)S(1)} %get-tuple-element.18.u_ref, ...), custom_call_target="tpu_custom_call" | custom-call | flops 16000000 | bytes 4000000 | tf_op jit(solution)/shard_map/bulk_fluxes/pallas_call | solution.py:239
  26.3 1.8 %collective-permute-done.1.west_ref = f32[6,8,128]{2,1,0:T(8,128)S(1)} collective-permute-done((f32[6,8,128]{2,1,0:T(8,128)S(1)}, f32[6,8,128]{2,1,0:T(8,128)S(1)}, u32[]{:S(2)}, u32[]{:S(2)}) %collective-permute-start.1) | collective-permute-done | bytes 24608 | tf_op jit(solution)/shard_map/ppermute | solution.py:416
  28.2 0.0 collective-permute-done.east_ref
  28.2 0.0 collective-permute-done.2.p1_ref
  28.2 0.0 collective-permute-done.3.p2_ref
  28.2 3.6 %solve_columns.1 = (f32[16,64,128]{2,1,0:T(8,128)}, f32[16,64,128]{2,1,0:T(8,128)}) custom-call(f32[16,64,128]{2,1,0:T(8,128)S(1)} %get-tuple-element.22.ts_ref, f32[16,64,128]{2,1,0:T(8,128)S(1)} %get-tuple-element.23.ss_ref, s32[64,128]{1,0:T(8,128)S(1)} %get-tuple-element.21.k_ref, f32[21,8,128]{2,1,0:T(8,128)S(1)} %get-tuple-element.24.own_ref, ...), custom_call_target="tpu_custom_call" | custom-call | flops 6000000 | bytes 2500000 | tf_op jit(solution)/shard_map/solve_columns/pallas_call | solution.py:384
Async XLA Ops:
  3.0 25.1 %collective-permute-start.2 = (f32[88,128]{1,0:T(8,128)S(1)}, f32[88,128]{1,0:T(8,128)S(1)}, u32[]{:S(2)}, u32[]{:S(2)}) collective-permute-start(f32[88,128]{1,0:T(8,128)S(1)} %get-tuple-element.27), channel_id=1, source_target_pairs={{0,32},{32,0},{64,96},{96,64},{128,160},{160,128},{192,224},{224,1... | collective-permute-start | bytes 135176 | tf_op jit(solution)/shard_map/ppermute | solution.py:414
  5.6 22.5 %collective-permute-start.3 = (f32[88,128]{1,0:T(8,128)S(1)}, f32[88,128]{1,0:T(8,128)S(1)}, u32[]{:S(2)}, u32[]{:S(2)}) collective-permute-start(f32[88,128]{1,0:T(8,128)S(1)} %get-tuple-element.28), channel_id=1, source_target_pairs={{32,64},{64,32},{96,128},{128,96},{160,192},{192,160},{224,256},{2... | collective-permute-start | bytes 135176 | tf_op jit(solution)/shard_map/ppermute | solution.py:415
  16.9 11.3 %collective-permute-start = (f32[7,8,128]{2,1,0:T(8,128)S(1)}, f32[7,8,128]{2,1,0:T(8,128)S(1)}, u32[]{:S(2)}, u32[]{:S(2)}) collective-permute-start(f32[7,8,128]{2,1,0:T(8,128)S(1)} %get-tuple-element.25), channel_id=1, source_target_pairs={{0,1},{1,2},{2,3},{3,4},{4,5},{5,6},{6,7},{7,8},{8,9},{9,10},{10,1... | collective-permute-start | bytes 86024 | tf_op jit(solution)/shard_map/ppermute | solution.py:413
  21.5 6.7 %collective-permute-start.1 = (f32[6,8,128]{2,1,0:T(8,128)S(1)}, f32[6,8,128]{2,1,0:T(8,128)S(1)}, u32[]{:S(2)}, u32[]{:S(2)}) collective-permute-start(f32[6,8,128]{2,1,0:T(8,128)S(1)} %get-tuple-element.26), channel_id=1, source_target_pairs={{1,0},{2,1},{3,2},{4,3},{5,4},{6,5},{7,6},{8,7},{9,8},{10,9},{11,1... | collective-permute-start | bytes 73736 | tf_op jit(solution)/shard_map/ppermute | solution.py:416

commit v2 on v1

--- a/solution.py
+++ b/solution.py
@@ -20,6 +20,7 @@
 NJ = 64
 NI = 128
 NB = NJ // 8
+SOLVE_ROWS = 32
 F32 = jnp.float32
 
 COLS = (-3, -2, -1, 0, 1, 2)
@@ -48,105 +49,9 @@
     return c_open * (jnp.where(up, qa, qb) + factor * jnp.where(up, sa, sb))
 
 
-def pack_kernel(
-    t_hbm, s_hbm, u_hbm, v_hbm, w_hbm, k_hbm, east_ref, west_ref, p1_ref, p2_ref, own_ref,
-    t_ref, s_ref, u_ref, v_ref, w_ref, k_ref, sems,
-):
-    chunks = 4
-    per = NK // chunks
-    copies = []
-    for c in range(chunks):
-        part = pl.ds(c * per, per)
-        for f, (src, dst) in enumerate(((t_hbm, t_ref), (s_hbm, s_ref), (u_hbm, u_ref))):
-            copies.append(pltpu.make_async_copy(src.at[part], dst.at[part], sems.at[c * 3 + f]))
-    late = [
-        pltpu.make_async_copy(k_hbm, k_ref, sems.at[12]),
-        pltpu.make_async_copy(v_hbm, v_ref, sems.at[13]),
-        pltpu.make_async_copy(w_hbm, w_ref, sems.at[14]),
-    ]
-    for c in copies + late:
-        c.start()
-
-    lane = lanes()
-    even = lax.rem(lax.axis_index("ja"), 2) == 0
-    near1 = jnp.where(even, NJ - 1, 0)
-    far1 = jnp.where(even, NJ - 2, 1)
-    near2 = jnp.where(even, 0, NJ - 1)
-    far2 = jnp.where(even, 1, NJ - 2)
-    rows = ((p1_ref, near1, far1), (p2_ref, near2, far2))
-
-    def windows(blocks, k, window):
-        out = pltpu.roll(blocks[0], k, 1)
-        for b in range(1, NB):
-            out = jnp.where(window == b, pltpu.roll(blocks[b], b * 16 + k, 1), out)
-        return out
-
-    t_acc = [None] * 6
-    s_acc = [None] * 6
-    u_acc = [None] * 6
-    for k in range(NK):
-        if k % per == 0:
-            for c in copies[k // per * 3 : k // per * 3 + 3]:
-                c.wait()
-        place = (lane - (k - 3)) & (NI - 1)
-        window = lax.shift_right_logical(place, 4)
-        within = place & 15
-        for ref, acc, which in ((t_ref, t_acc, range(6)), (s_ref, s_acc, range(6)), (u_ref, u_acc, (1, 2, 3))):
-            got = windows([ref[k, pl.ds(8 * b, 8), :] for b in range(NB)], k, window)
-            for n in which:
-                acc[n] = got if k == 0 else jnp.where(within == n, got, acc[n])
-        for ref, near, far in rows:
-            ref[pl.ds(k, 1), :] = t_ref[k, pl.ds(near, 1), :]
-            ref[pl.ds(16 + k, 1), :] = t_ref[k, pl.ds(far, 1), :]
-            ref[pl.ds(32 + k, 1), :] = s_ref[k, pl.ds(near, 1), :]
-            ref[pl.ds(48 + k, 1), :] = s_ref[k, pl.ds(far, 1), :]
-    for c in late:
-        c.wait()
-    for ref, near, far in rows:
-        for k in range(NK):
-            ref[pl.ds(64 + k, 1), :] = v_ref[k, pl.ds(near, 1), :]
-        ref[pl.ds(80, 8), :] = jnp.zeros((8, NI), F32)
-        ref[pl.ds(80, 1), :] = k_ref[pl.ds(near, 1), :].astype(F32)
-        ref[pl.ds(81, 1), :] = k_ref[pl.ds(far, 1), :].astype(F32)
-
-    place = (lane + 3) & (NI - 1)
-    floor = windows([k_ref[pl.ds(8 * b, 8), :].astype(F32) for b in range(NB)], 0, lax.shift_right_logical(place, 4))
-    first = (lane & 15) == 0
-    k_cols = []
-    for n, off in enumerate(COLS):
-        x = jnp.where(first, pltpu.roll(floor, -off % NI, 1), 0.0)
-        for step in (1, 2, 4, 8):
-            x = x + pltpu.roll(x, step, 1)
-        k_cols.append(x)
-    t_cols = [pltpu.roll(x, -off % NI, 1) for x, off in zip(t_acc, COLS)]
-    s_cols = [pltpu.roll(x, -off % NI, 1) for x, off in zip(s_acc, COLS)]
-    u_cols = [pltpu.roll(u_acc[n], -COLS[n] % NI, 1) for n in (1, 2, 3)]
-    for n, x in enumerate(t_cols + s_cols + k_cols + u_cols):
-        own_ref[n] = x
-    for n, x in enumerate((t_cols[2], t_cols[1], s_cols[2], s_cols[1], k_cols[2], k_cols[1], u_cols[1])):
-        east_ref[n] = x
-    for n, x in enumerate((t_cols[3], t_cols[4], s_cols[3], s_cols[4], k_cols[3], k_cols[4])):
-        west_ref[n] = x
-
-
-def pack(t, s, u, v, w, floor):
-    fields = [pltpu.with_memory_space_constraint(x, pltpu.HBM) for x in (t, s, u, v, w, floor)]
-    return pl.pallas_call(
-        pack_kernel,
-        out_shape=tuple(
-            pltpu.VMEM(shape, F32) for shape in ((7, 8, NI), (6, 8, NI), (MROWS, NI), (MROWS, NI), (21, 8, NI))
-        )
-        + (pltpu.VMEM((NK, NJ, NI), F32),) * 5
-        + (pltpu.VMEM((NJ, NI), jnp.int32),),
-        in_specs=[pl.BlockSpec(memory_space=pltpu.HBM)] * 6,
-        out_specs=(pl.BlockSpec(memory_space=pltpu.VMEM),) * 11,
-        scratch_shapes=[pltpu.SemaphoreType.DMA((15,))],
-        compiler_params=pltpu.CompilerParams(vmem_limit_bytes=16 * 2**20),
-        name="pack_edges",
-    )(*fields)
-
-
-def bulk_kernel(t_ref, s_ref, u_ref, v_ref, w_ref, k_ref, to_ref, so_ref, rows_ref, th_ref, sh_ref, mask_ref):
+def bulk_fluxes(t_ref, s_ref, u_ref, v_ref, w_hbm, k_ref, to_ref, so_ref, w_ref, th_ref, sh_ref, mask_ref, sem):
+    w_copy = pltpu.make_async_copy(w_hbm, w_ref, sem)
+    w_copy.start()
     lane = lanes()
     sub = sublanes()
     floors = [k_ref[pl.ds(m, 8, stride=8), :] for m in range(NB)]
@@ -199,6 +104,8 @@
     def _(k):
         level(k)
 
+    w_copy.wait()
+
     def column(b, _):
         at = pl.ds(pl.multiple_of(b * 8, 8), 8)
         floor = k_ref[at, :]
@@ -224,32 +131,119 @@
 
     lax.fori_loop(0, NB, column, 0)
 
-    for n, r in enumerate(ROWS):
+
+def bulk_scratch():
+    field = pltpu.VMEM((NK, NJ, NI), F32)
+    return [field, field, field, pltpu.VMEM((4, NB, 8, NI), jnp.int32), pltpu.SemaphoreType.DMA(())]
+
+
+def bulk_first():
+    ja, ia = lax.axis_index("ja"), lax.axis_index("ia")
+    ni = lax.axis_size("ia")
+    near_fold = ja >= lax.axis_size("ja") - 2
+    return ia < jnp.where(near_fold, 3 * ni // 8, ni // 8)
+
+
+def pack_kernel(
+    t_hbm, s_hbm, u_hbm, v_hbm, w_hbm, k_hbm, p2_ref, east_ref, west_ref, p1_ref, own_ref,
+    t_ref, s_ref, u_ref, v_ref, k_ref, ts_ref, ss_ref, sems, *scratch,
+):
+    chunks = 4
+    per = NK // chunks
+    copies = []
+    for c in range(chunks):
+        part = pl.ds(c * per, per)
+        for f, (src, dst) in enumerate(((t_hbm, t_ref), (s_hbm, s_ref), (u_hbm, u_ref))):
+            copies.append(pltpu.make_async_copy(src.at[part], dst.at[part], sems.at[c * 3 + f]))
+    early = [
+        pltpu.make_async_copy(k_hbm, k_ref, sems.at[12]),
+        pltpu.make_async_copy(v_hbm, v_ref, sems.at[13]),
+    ]
+    for c in early + copies:
+        c.start()
+
+    lane = lanes()
+    even = lax.rem(lax.axis_index("ja"), 2) == 0
+    near1 = jnp.where(even, NJ - 1, 0)
+    far1 = jnp.where(even, NJ - 2, 1)
+    near2 = jnp.where(even, 0, NJ - 1)
+    far2 = jnp.where(even, 1, NJ - 2)
+    rows = ((p1_ref, near1, far1), (p2_ref, near2, far2))
+
+    def windows(blocks, k, window):
+        out = pltpu.roll(blocks[0], k, 1)
+        for b in range(1, NB):
+            out = jnp.where(window == b, pltpu.roll(blocks[b], b * 16 + k, 1), out)
+        return out
+
+    early[0].wait()
+    place = (lane + 3) & (NI - 1)
+    floor = windows([k_ref[pl.ds(8 * b, 8), :].astype(F32) for b in range(NB)], 0, lax.shift_right_logical(place, 4))
+    first = (lane & 15) == 0
+    k_cols = []
+    for n, off in enumerate(COLS):
+        x = jnp.where(first, pltpu.roll(floor, -off % NI, 1), 0.0)
+        for step in (1, 2, 4, 8):
+            x = x + pltpu.roll(x, step, 1)
+        k_cols.append(x)
+    early[1].wait()
+    for ref, near, far in rows:
         for k in range(NK):
-            rows_ref[n, pl.ds(k, 1), :] = t_ref[k, pl.ds(r, 1), :]
-            rows_ref[6 + n, pl.ds(k, 1), :] = s_ref[k, pl.ds(r, 1), :]
-    for n, r in enumerate((0, 62, 63)):
-        for k in range(NK):
-            rows_ref[12 + n, pl.ds(k, 1), :] = v_ref[k, pl.ds(r, 1), :]
-
-
-def bulk(t, s, u, v, w, floor):
-    vmem = pl.BlockSpec(memory_space=pltpu.VMEM)
-    field = pltpu.VMEM((NK, NJ, NI), F32)
+            ref[pl.ds(64 + k, 1), :] = v_ref[k, pl.ds(near, 1), :]
+        ref[pl.ds(80, 8), :] = jnp.zeros((8, NI), F32)
+        ref[pl.ds(80, 1), :] = k_ref[pl.ds(near, 1), :].astype(F32)
+        ref[pl.ds(81, 1), :] = k_ref[pl.ds(far, 1), :].astype(F32)
+
+    t_acc = [None] * 6
+    s_acc = [None] * 6
+    u_acc = [None] * 6
+    for k in range(NK):
+        if k % per == 0:
+            for c in copies[k // per * 3 : k // per * 3 + 3]:
+                c.wait()
+        place = (lane - (k - 3)) & (NI - 1)
+        window = lax.shift_right_logical(place, 4)
+        within = place & 15
+        for ref, acc, which in ((t_ref, t_acc, range(6)), (s_ref, s_acc, range(6)), (u_ref, u_acc, (1, 2, 3))):
+            got = windows([ref[k, pl.ds(8 * b, 8), :] for b in range(NB)], k, window)
+            for n in which:
+                acc[n] = got if k == 0 else jnp.where(within == n, got, acc[n])
+        for ref, near, far in rows:
+            ref[pl.ds(k, 1), :] = t_ref[k, pl.ds(near, 1), :]
+            ref[pl.ds(16 + k, 1), :] = t_ref[k, pl.ds(far, 1), :]
+            ref[pl.ds(32 + k, 1), :] = s_ref[k, pl.ds(near, 1), :]
+            ref[pl.ds(48 + k, 1), :] = s_ref[k, pl.ds(far, 1), :]
+    t_cols = [pltpu.roll(x, -off % NI, 1) for x, off in zip(t_acc, COLS)]
+    s_cols = [pltpu.roll(x, -off % NI, 1) for x, off in zip(s_acc, COLS)]
+    u_cols = [pltpu.roll(u_acc[n], -COLS[n] % NI, 1) for n in (1, 2, 3)]
+    for n, x in enumerate(t_cols + s_cols + k_cols + u_cols):
+        own_ref[n] = x
+    for n, x in enumerate((t_cols[2], t_cols[1], s_cols[2], s_cols[1], k_cols[2], k_cols[1], u_cols[1])):
+        east_ref[n] = x
+    for n, x in enumerate((t_cols[3], t_cols[4], s_cols[3], s_cols[4], k_cols[3], k_cols[4])):
+        west_ref[n] = x
+
+    @pl.when(bulk_first())
+    def _():
+        bulk_fluxes(t_ref, s_ref, u_ref, v_ref, w_hbm, k_ref, ts_ref, ss_ref, *scratch)
+
+
+def pack(t, s, u, v, w, floor):
+    fields = [pltpu.with_memory_space_constraint(x, pltpu.HBM) for x in (t, s, u, v, w, floor)]
     return pl.pallas_call(
-        bulk_kernel,
-        out_shape=(
-            pltpu.VMEM((NK, NJ, NI), F32),
-            pltpu.VMEM((NK, NJ, NI), F32),
-            pltpu.VMEM((15, NK, NI), F32),
-        ),
-        in_specs=[vmem] * 6,
-        out_specs=(vmem,) * 3,
-        scratch_shapes=[field, field, pltpu.VMEM((4, NB, 8, NI), jnp.int32)],
+        pack_kernel,
+        out_shape=tuple(
+            pltpu.VMEM(shape, F32) for shape in ((MROWS, NI), (11, 8, NI), (11, 8, NI), (MROWS, NI), (21, 8, NI))
+        )
+        + (pltpu.VMEM((NK, NJ, NI), F32),) * 4
+        + (pltpu.VMEM((NJ, NI), jnp.int32),)
+        + (pltpu.VMEM((NK, NJ, NI), F32),) * 2,
+        in_specs=[pl.BlockSpec(memory_space=pltpu.HBM)] * 6,
+        out_specs=(pl.BlockSpec(memory_space=pltpu.VMEM),) * 12,
+        scratch_shapes=[pltpu.SemaphoreType.DMA((14,))] + bulk_scratch(),
         compiler_params=pltpu.CompilerParams(vmem_limit_bytes=16 * 2**20),
-        cost_estimate=pl.CostEstimate(flops=16_000_000, bytes_accessed=4_000_000, transcendentals=0),
-        name="bulk_fluxes",
-    )(t, s, u, v, w, floor)
+        name="pack_edges",
+    )(*fields)
 
 
 def edge_fluxes(level, q, floor, c):
@@ -263,9 +257,23 @@
 
 
 def solve_kernel(
-    ts_ref, ss_ref, k_ref, own_ref, east_ref, west_ref, p1_ref, p2_ref, rows_ref, tn_hbm, sn_hbm,
-    to_ref, so_ref, zonal_ref, merid_ref, out_sems,
+    t_ref, s_ref, u_ref, v_ref, w_hbm, k_ref, ts_in, ss_in, own_ref,
+    p2_ref, east_ref, west_ref, p1_ref, tn_hbm, sn_hbm,
+    ts_ref, ss_ref, to_ref, so_ref, zonal_ref, merid_ref, rows_ref, out_sems, *scratch,
 ):
+    done_first = bulk_first()
+
+    @pl.when(jnp.logical_not(done_first))
+    def _():
+        bulk_fluxes(t_ref, s_ref, u_ref, v_ref, w_hbm, k_ref, ts_ref, ss_ref, *scratch)
+
+    for k in range(NK):
+        for n, r in enumerate(ROWS):
+            rows_ref[n, pl.ds(k, 1), :] = t_ref[k, pl.ds(r, 1), :]
+            rows_ref[6 + n, pl.ds(k, 1), :] = s_ref[k, pl.ds(r, 1), :]
+        for n, r in enumerate((0, 62, 63)):
+            rows_ref[12 + n, pl.ds(k, 1), :] = v_ref[k, pl.ds(r, 1), :]
+
     lane = lanes()
     ja = lax.axis_index("ja")
     even = lax.rem(ja, 2) == 0
@@ -317,18 +325,31 @@
 
     edge_lanes = (lane < 2) | (lane >= NI - 2)
 
+    def block(b):
+        return pl.ds(pl.multiple_of(b * SOLVE_ROWS, SOLVE_ROWS), SOLVE_ROWS)
+
+    def out_copies(b):
+        at = block(b)
+        return [
+            pltpu.make_async_copy(to_ref.at[:, at], tn_hbm.at[:, at], out_sems.at[0, b]),
+            pltpu.make_async_copy(so_ref.at[:, at], sn_hbm.at[:, at], out_sems.at[1, b]),
+        ]
+
     def column(b, _):
-        at = pl.ds(pl.multiple_of(b * 8, 8), 8)
-        side = jnp.where(b == 0, 0, jnp.where(b == NB - 1, 2, 1))
+        at = block(b)
         floor = k_ref[at, :]
         wet = [floor > k for k in range(NK)]
         star = []
-        for n, ref in enumerate((ts_ref, ss_ref)):
+        for n, (first, ref) in enumerate(((ts_in, ts_ref), (ss_in, ss_ref))):
             star.append([])
             for k in range(NK):
-                amount = lax.rem(2 * NI - 2 - 4 * (k // 4) - 16 * b, NI)
-                z = pltpu.roll(zonal_ref[n, k % 4], amount, 1)
-                x = ref[k, at, :] - (jnp.where(edge_lanes, z, 0.0) + merid_ref[n, side, k])
+                corrections = []
+                for h in range(SOLVE_ROWS // 8):
+                    c = b * (SOLVE_ROWS // 8) + h
+                    z = pltpu.roll(zonal_ref[n, k % 4], lax.rem(2 * NI - 2 - 4 * (k // 4) - 16 * c, NI), 1)
+                    side = jnp.where(c == 0, 0, jnp.where(c == NB - 1, 2, 1))
+                    corrections.append(jnp.where(edge_lanes, z, 0.0) + merid_ref[n, side, k])
+                x = jnp.where(done_first, first[k, at, :], ref[k, at, :]) - jnp.concatenate(corrections, axis=0)
                 star[n].append(jnp.where(wet[k], x, 0.0))
         dens = []
         for k in range(NK):
@@ -366,42 +387,42 @@
             for k in range(NK - 2, -1, -1):
                 x = values[n][k] + ratio[k] * x
                 out[k, at, :] = jnp.where(wet[k], x, 0.0)
-        pltpu.make_async_copy(to_ref.at[:, at], tn_hbm.at[:, at], out_sems.at[0, b]).start()
-        pltpu.make_async_copy(so_ref.at[:, at], sn_hbm.at[:, at], out_sems.at[1, b]).start()
+        for c in out_copies(b):
+            c.start()
         return 0
 
-    lax.fori_loop(0, NB, column, 0)
-    for b in range(NB):
-        at = pl.ds(b * 8, 8)
-        pltpu.make_async_copy(to_ref.at[:, at], tn_hbm.at[:, at], out_sems.at[0, b]).wait()
-        pltpu.make_async_copy(so_ref.at[:, at], sn_hbm.at[:, at], out_sems.at[1, b]).wait()
-
-
-def solve(ts, ss, floor, own, east, west, p1, p2, rows):
-    any_ = pl.BlockSpec(memory_space=pltpu.HBM)
+    lax.fori_loop(0, NJ // SOLVE_ROWS, column, 0)
+    for b in range(NJ // SOLVE_ROWS):
+        for c in out_copies(b):
+            c.wait()
+
+
+def solve(t, s, u, v, w, floor, ts, ss, *edges):
     vmem = pl.BlockSpec(memory_space=pltpu.VMEM)
+    hbm = pl.BlockSpec(memory_space=pltpu.HBM)
     field = pltpu.VMEM((NK, NJ, NI), F32)
+    w = pltpu.with_memory_space_constraint(w, pltpu.HBM)
     return pl.pallas_call(
         solve_kernel,
         out_shape=(jax.ShapeDtypeStruct((NK, NJ, NI), F32),) * 2,
-        in_specs=[vmem] * 9,
-        out_specs=(any_, any_),
-        scratch_shapes=[field] * 2
+        in_specs=[vmem] * 4 + [hbm] + [vmem] * (3 + len(edges)),
+        out_specs=(hbm, hbm),
+        scratch_shapes=[field] * 4
         + [
             pltpu.VMEM((2, 4, 8, NI), F32),
             pltpu.VMEM((2, 3, NK, 8, NI), F32),
+            pltpu.VMEM((15, NK, NI), F32),
             pltpu.SemaphoreType.DMA((2, NB)),
-        ],
-        compiler_params=pltpu.CompilerParams(vmem_limit_bytes=16 * 2**20),
+        ]
+        + bulk_scratch(),
+        compiler_params=pltpu.CompilerParams(vmem_limit_bytes=24 * 2**20),
         cost_estimate=pl.CostEstimate(flops=6_000_000, bytes_accessed=2_500_000, transcendentals=300_000),
         name="solve_columns",
-    )(ts, ss, floor, own, east, west, p1, p2, rows)
+    )(t, s, u, v, w, floor, ts, ss, *edges)
 
 
 def local(nj, ni, t, s, u, v, w, floor):
-    east, west, p1, p2, own, t, s, u, v, w, floor = pack(t, s, u, v, w, floor)
-    east_pairs = [(i, (i + 1) % ni) for i in range(ni)]
-    west_pairs = [((i + 1) % ni, i) for i in range(ni)]
+    p2, east, west, p1, own, t, s, u, v, floor, ts, ss = pack(t, s, u, v, w, floor)
     first = []
     second = []
     for i in range(ni):
@@ -410,12 +431,11 @@
         for j in range(1, nj - 1, 2):
             second += [(j * ni + i, (j + 1) * ni + i), ((j + 1) * ni + i, j * ni + i)]
         second.append(((nj - 1) * ni + i, (nj - 1) * ni + ni - 1 - i))
-    from_west = lax.ppermute(east, "ia", east_pairs)
-    q1 = lax.ppermute(p1, ("ja", "ia"), first)
-    q2 = lax.ppermute(p2, ("ja", "ia"), second)
-    from_east = lax.ppermute(west, "ia", west_pairs)
-    ts, ss, rows = bulk(t, s, u, v, w, floor)
-    return solve(ts, ss, floor, own, from_west, from_east, q1, q2, rows)
+    p1 = lax.ppermute(p1, ("ja", "ia"), first)
+    p2 = lax.ppermute(p2, ("ja", "ia"), second)
+    from_west = lax.ppermute(east, "ia", [(i, (i + 1) % ni) for i in range(ni)])
+    from_east = lax.ppermute(west, "ia", [((i + 1) % ni, i) for i in range(ni)])
+    return solve(t, s, u, v, w, floor, ts, ss, own, p2, from_west, from_east, p1)
 
 
 def solution(mesh):

time: 32 us -> 28 us (0.88)
  starting transfers between devices: 20.3 us -> 16.9 us
  Pallas kernels: 8.94 us -> 7.18 us
  waiting for transfers between devices: 1.82 us -> 3.03 us
    ppermute x4, starting transfers between devices: 20.3 us -> 16.9 us  [the longest x1 8.47 us: local(): p2 = lax.ppermute(p2, ('ja', 'ia'), second)]
    pallas_call x1 -> x0, Pallas kernels: 2.93 us -> none  [bulk(): pl.pallas_call(bulk_kernel, out_shape=(pltpu.VMEM((NK, NJ, NI), F32), plt...]
    pallas_call x1, Pallas kernels: 2.39 us -> 4.98 us  [pack(): pl.pallas_call(pack_kernel, out_shape=tuple((pltpu.VMEM(shape, F32) for s...]
    pallas_call x1, Pallas kernels: 3.62 us -> 2.2 us  [solve(): pl.pallas_call(solve_kernel, out_shape=(jax.ShapeDtypeStruct((NK, NJ, NI)...]
    ppermute x4, waiting for transfers between devices: 1.82 us -> 3.03 us  [the longest x1 3.02 us: local(): from_east = lax.ppermute(west, 'ia', [((i + 1) % ni, i) for i in range(ni)])]
  transfers between devices with their start and end apart: 4 -> 4, of which waited for: 1 -> 1; matrix products, arithmetic and copies ran while one was open for 0% -> 0% of each run, Pallas kernels for 9% -> 0%
where the time goes in v2:
time: 28 us; the launch traced here: 27.8 us
  starting transfers between devices  16.9 us (60%)
  Pallas kernels  7.18 us (26%)
  waiting for transfers between devices  3.03 us (11%)
  between operations  0.69 us (2%)
    ppermute x1, starting transfers between devices, local(): p2 = lax.ppermute(p2, ('ja', 'ia'), second)  8.47 us
    pallas_call x1, Pallas kernels, pack(): pl.pallas_call(pack_kernel, out_shape=tuple((pltpu.VMEM(shape, F32) for s...  4.98 us
    ppermute x1, starting transfers between devices, local(): from_west = lax.ppermute(east, 'ia', [(i, (i + 1) % ni) for i in range(ni)])  4.57 us
    ppermute x1, waiting for transfers between devices, local(): from_east = lax.ppermute(west, 'ia', [((i + 1) % ni, i) for i in range(ni)])  3.02 us
    pallas_call x1, Pallas kernels, solve(): pl.pallas_call(solve_kernel, out_shape=(jax.ShapeDtypeStruct((NK, NJ, NI)...  2.2 us
    ppermute x1, starting transfers between devices, local(): from_east = lax.ppermute(west, 'ia', [((i + 1) % ni, i) for i in range(ni)])  1.92 us
    ppermute x1, starting transfers between devices, local(): p1 = lax.ppermute(p1, ('ja', 'ia'), first)  1.92 us
  transfers between devices with their start and end apart: 4, of which 1 were waited for; matrix products, arithmetic and copies ran while one was open for 0% of the time, Pallas kernels for 0%

profile of v2, /device:TPU:127, one launch (start us, length us, event | category | flops | bytes accessed | tf_op | source)
XLA Modules:
  0.0 27.8 jit_solution(14990662931547200846)
XLA Ops:
  0.6 5.0 %pack_edges.1 = (f32[88,128]{1,0:T(8,128)S(1)}, f32[11,8,128]{2,1,0:T(8,128)S(1)}, f32[11,8,128]{2,1,0:T(8,128)S(1)}, f32[88,128]{1,0:T(8,128)S(1)}, f32[21,8,12...) custom-call(f32[16,64,128]{2,1,0:T(8,128)} %t_hbm.1, ...), custom_call_target="tpu_custom_call" | custom-call | tf_op jit(solution)/shard_map/pack_edges/pallas_call | solution.py:233
  5.6 8.5 %collective-permute-start = (f32[88,128]{1,0:T(8,128)S(1)}, f32[88,128]{1,0:T(8,128)S(1)}, u32[]{:S(2)}, u32[]{:S(2)}) collective-permute-start(f32[88,128]{1,0:T(8,128)S(1)} %get-tuple-element.22), channel_id=1, source_target_pairs={{32,64},{64,32},{96,128},{128,96},{160,192},{192,160},{224,256},{2... | collective-permute-start | bytes 135176 | tf_op jit(solution)/shard_map/ppermute | solution.py:435
  14.1 4.6 %collective-permute-start.1 = (f32[11,8,128]{2,1,0:T(8,128)S(1)}, f32[11,8,128]{2,1,0:T(8,128)S(1)}, u32[]{:S(2)}, u32[]{:S(2)}) collective-permute-start(f32[11,8,128]{2,1,0:T(8,128)S(1)} %get-tuple-element.23), channel_id=1, source_target_pairs={{0,1},{1,2},{2,3},{3,4},{4,5},{5,6},{6,7},{7,8},{8,9},{9,10},{10,1... | collective-permute-start | bytes 135176 | tf_op jit(solution)/shard_map/ppermute | solution.py:436
  18.7 1.9 %collective-permute-start.2 = (f32[11,8,128]{2,1,0:T(8,128)S(1)}, f32[11,8,128]{2,1,0:T(8,128)S(1)}, u32[]{:S(2)}, u32[]{:S(2)}) collective-permute-start(f32[11,8,128]{2,1,0:T(8,128)S(1)} %get-tuple-element.24), channel_id=1, source_target_pairs={{1,0},{2,1},{3,2},{4,3},{5,4},{6,5},{7,6},{8,7},{9,8},{10,9},{11,1... | collective-permute-start | bytes 135176 | tf_op jit(solution)/shard_map/ppermute | solution.py:437
  20.6 1.9 %collective-permute-start.3 = (f32[88,128]{1,0:T(8,128)S(1)}, f32[88,128]{1,0:T(8,128)S(1)}, u32[]{:S(2)}, u32[]{:S(2)}) collective-permute-start(f32[88,128]{1,0:T(8,128)S(1)} %get-tuple-element.25), channel_id=1, source_target_pairs={{0,32},{32,0},{64,96},{96,64},{128,160},{160,128},{192,224},{224,1... | collective-permute-start | bytes 135176 | tf_op jit(solution)/shard_map/ppermute | solution.py:434
  22.5 0.0 collective-permute-done.p2_ref
  22.5 0.0 collective-permute-done.1.east_ref
  22.6 3.0 %collective-permute-done.2.west_ref = f32[11,8,128]{2,1,0:T(8,128)S(1)} collective-permute-done((f32[11,8,128]{2,1,0:T(8,128)S(1)}, f32[11,8,128]{2,1,0:T(8,128)S(1)}, u32[]{:S(2)}, u32[]{:S(2)}) %collective-permute-start.2) | collective-permute-done | bytes 45088 | tf_op jit(solution)/shard_map/ppermute | solution.py:437
  25.6 0.0 collective-permute-done.3.p1_ref
  25.6 2.2 %solve_columns.1 = (f32[16,64,128]{2,1,0:T(8,128)}, f32[16,64,128]{2,1,0:T(8,128)}) custom-call(f32[16,64,128]{2,1,0:T(8,128)S(1)} %get-tuple-element.14.t_ref, f32[16,64,128]{2,1,0:T(8,128)S(1)} %get-tuple-element.15.s_ref, f32[16,64,128]{2,1,0:T(8,128)S(1)} %get-tuple-element.16.u_ref, f32[16,64,128]{2,1,0:T(8,128)S(1)} %get-tuple-element.17.v_ref, ...), custom_call_target="tpu_custom_call" | custom-call | flops 6000000 | bytes 2500000 | tf_op jit(solution)/shard_map/solve_columns/pallas_call | solution.py:405
Async XLA Ops:
  5.6 16.9 %collective-permute-start = (f32[88,128]{1,0:T(8,128)S(1)}, f32[88,128]{1,0:T(8,128)S(1)}, u32[]{:S(2)}, u32[]{:S(2)}) collective-permute-start(f32[88,128]{1,0:T(8,128)S(1)} %get-tuple-element.22), channel_id=1, source_target_pairs={{32,64},{64,32},{96,128},{128,96},{160,192},{192,160},{224,256},{2... | collective-permute-start | bytes 135176 | tf_op jit(solution)/shard_map/ppermute | solution.py:435
  14.1 8.4 %collective-permute-start.1 = (f32[11,8,128]{2,1,0:T(8,128)S(1)}, f32[11,8,128]{2,1,0:T(8,128)S(1)}, u32[]{:S(2)}, u32[]{:S(2)}) collective-permute-start(f32[11,8,128]{2,1,0:T(8,128)S(1)} %get-tuple-element.23), channel_id=1, source_target_pairs={{0,1},{1,2},{2,3},{3,4},{4,5},{5,6},{6,7},{7,8},{8,9},{9,10},{10,1... | collective-permute-start | bytes 135176 | tf_op jit(solution)/shard_map/ppermute | solution.py:436
  18.7 6.9 %collective-permute-start.2 = (f32[11,8,128]{2,1,0:T(8,128)S(1)}, f32[11,8,128]{2,1,0:T(8,128)S(1)}, u32[]{:S(2)}, u32[]{:S(2)}) collective-permute-start(f32[11,8,128]{2,1,0:T(8,128)S(1)} %get-tuple-element.24), channel_id=1, source_target_pairs={{1,0},{2,1},{3,2},{4,3},{5,4},{6,5},{7,6},{8,7},{9,8},{10,9},{11,1... | collective-permute-start | bytes 135176 | tf_op jit(solution)/shard_map/ppermute | solution.py:437
  20.6 5.0 %collective-permute-start.3 = (f32[88,128]{1,0:T(8,128)S(1)}, f32[88,128]{1,0:T(8,128)S(1)}, u32[]{:S(2)}, u32[]{:S(2)}) collective-permute-start(f32[88,128]{1,0:T(8,128)S(1)} %get-tuple-element.25), channel_id=1, source_target_pairs={{0,32},{32,0},{64,96},{96,64},{128,160},{160,128},{192,224},{224,1... | collective-permute-start | bytes 135176 | tf_op jit(solution)/shard_map/ppermute | solution.py:434

commit v3 on v2

--- a/solution.py
+++ b/solution.py
@@ -20,11 +20,10 @@
 NJ = 64
 NI = 128
 NB = NJ // 8
-SOLVE_ROWS = 32
+HALF = NJ // 2
 F32 = jnp.float32
 
 COLS = (-3, -2, -1, 0, 1, 2)
-ROWS = (0, 1, 2, 61, 62, 63)
 MROWS = 88
 
 
@@ -256,10 +255,112 @@
     return out
 
 
-def solve_kernel(
-    t_ref, s_ref, u_ref, v_ref, w_hbm, k_ref, ts_in, ss_in, own_ref,
-    p2_ref, east_ref, west_ref, p1_ref, tn_hbm, sn_hbm,
-    ts_ref, ss_ref, to_ref, so_ref, zonal_ref, merid_ref, rows_ref, out_sems, *scratch,
+def solve_rows(south, folded, t_ref, s_ref, v_ref, k_ref, msg_ref, zonal_ref, stars, outs, rows_ref, merid_ref):
+    lane = lanes()
+    base = jnp.where(south, 0, NJ - 3)
+    for k in range(NK):
+        for n, ref in enumerate((t_ref, s_ref, v_ref)):
+            for r in range(3):
+                rows_ref[3 * n + r, pl.ds(k, 1), :] = ref[k, pl.ds(base + r, 1), :]
+
+    level = lax.broadcasted_iota(jnp.int32, (NK, NI), 0).astype(F32)
+    msg = [msg_ref[pl.ds(8 * n, 8), :] for n in range(MROWS // 8)]
+    if folded is not None:
+        turned = NI - 1 - lane
+        msg = [jnp.where(folded, jnp.take_along_axis(x, turned, axis=1), x) for x in msg]
+
+    def plane(n):
+        return jnp.concatenate([msg[2 * n], msg[2 * n + 1]], axis=0)
+
+    def wide(row):
+        return jnp.broadcast_to(row, (NK, NI))
+
+    def in_order(own, near, far):
+        return [jnp.where(south, x, y) for x, y in zip([far, near] + own, own + [near, far])]
+
+    floors = in_order([wide(k_ref[pl.ds(base + r, 1), :].astype(F32)) for r in range(3)], wide(msg[10][0:1]), wide(msg[10][1:2]))
+    last = rows_ref[8]
+    if folded is not None:
+        last = jnp.where(folded, 0.5 * (last - plane(4)), last)
+    courant = (jnp.where(south, plane(4), rows_ref[7]), jnp.where(south, rows_ref[6], last))
+    merid_ref[...] = jnp.zeros_like(merid_ref)
+    at_row = jnp.where(south, 0, 6)
+    for n in range(2):
+        q = in_order([rows_ref[3 * n + r] for r in range(3)], plane(2 * n), plane(2 * n + 1))
+        f0, f1 = edge_fluxes(level, q, floors, courant)
+        for i, x in enumerate((jnp.where(south, f1 - f0, f0), jnp.where(south, -f1, f1 - f0))):
+            for k in range(NK):
+                merid_ref[n, k, pl.ds(at_row + i, 1), :] = x[k : k + 1]
+
+    edge_lanes = (lane < 2) | (lane >= NI - 2)
+    half = jnp.where(south, 0, 1)
+    at = half_rows(south)
+    floor = k_ref[at, :]
+    wet = [floor > k for k in range(NK)]
+    star = []
+    for n in range(2):
+        star.append([])
+        for k in range(NK):
+            corrections = []
+            for h in range(HALF // 8):
+                c = half * (HALF // 8) + h
+                z = pltpu.roll(zonal_ref[n, k % 4], lax.rem(2 * NI - 2 - 4 * (k // 4) - 16 * c, NI), 1)
+                z = jnp.where(edge_lanes, z, 0.0)
+                if h == 0:
+                    z = z + jnp.where(south, merid_ref[n, k], 0.0)
+                if h == HALF // 8 - 1:
+                    z = z + jnp.where(south, 0.0, merid_ref[n, k])
+                corrections.append(z)
+            star[n].append(jnp.where(wet[k], stars(n, k, at) - jnp.concatenate(corrections, axis=0), 0.0))
+    dens = []
+    for k in range(NK):
+        z = LAYER_DEPTH * (k + 0.5)
+        ta = star[0][k] - 10.0
+        sa = star[1][k] - 35.0
+        heat = (-0.5 * THERMAL_COEF * CABBELING_T) * ta - MIXED_COEF * sa - THERMAL_COEF * (1.0 + THERMOBARIC_T * z)
+        salt = (-0.5 * HALINE_COEF * CABBELING_S) * sa + HALINE_COEF * (1.0 - THERMOBARIC_S * z)
+        dens.append(heat * ta + salt * sa)
+    above = None
+    ratio = []
+    values = ([], [])
+    for k in range(NK):
+        if k < NK - 1:
+            below = jnp.where(wet[k + 1], 5.5 - 5.0 * jnp.tanh(dens[k + 1] - dens[k]), 0.0)
+            pivot = 1.0 + below
+        else:
+            below = None
+            pivot = 1.0
+        if k > 0:
+            pivot = pivot + above * (1.0 - ratio[-1])
+        r = pl.reciprocal(pivot, approx=True)
+        r = r * (2.0 - pivot * r)
+        if below is not None:
+            ratio.append(below * r)
+        for n in range(2):
+            x = star[n][k]
+            if k > 0:
+                x = x + above * values[n][-1]
+            values[n].append(x * r)
+        above = below
+    for n in range(2):
+        x = values[n][NK - 1]
+        outs[n][NK - 1] = jnp.where(wet[NK - 1], x, 0.0)
+        for k in range(NK - 2, -1, -1):
+            x = values[n][k] + ratio[k] * x
+            outs[n][k] = jnp.where(wet[k], x, 0.0)
+
+
+def half_rows(south):
+    return pl.ds(pl.multiple_of(jnp.where(south, 0, HALF), HALF), HALF)
+
+
+def even_row():
+    return lax.rem(lax.axis_index("ja"), 2) == 0
+
+
+def first_kernel(
+    t_ref, s_ref, u_ref, v_ref, w_hbm, k_ref, ts_in, ss_in, own_ref, east_ref, p2_ref, west_ref,
+    tn_ref, sn_ref, ts_ref, ss_ref, zonal_ref, rows_ref, merid_ref, *scratch,
 ):
     done_first = bulk_first()
 
@@ -267,18 +368,7 @@
     def _():
         bulk_fluxes(t_ref, s_ref, u_ref, v_ref, w_hbm, k_ref, ts_ref, ss_ref, *scratch)
 
-    for k in range(NK):
-        for n, r in enumerate(ROWS):
-            rows_ref[n, pl.ds(k, 1), :] = t_ref[k, pl.ds(r, 1), :]
-            rows_ref[6 + n, pl.ds(k, 1), :] = s_ref[k, pl.ds(r, 1), :]
-        for n, r in enumerate((0, 62, 63)):
-            rows_ref[12 + n, pl.ds(k, 1), :] = v_ref[k, pl.ds(r, 1), :]
-
     lane = lanes()
-    ja = lax.axis_index("ja")
-    even = lax.rem(ja, 2) == 0
-    is_north = ja == lax.axis_size("ja") - 1
-
     level = (lane & 15).astype(F32)
     own = [own_ref[n] for n in range(21)]
     k_own = own[12:18]
@@ -297,128 +387,73 @@
                 x = jnp.where((lane & 3) == i, moved, x)
             zonal_ref[n, r] = x
 
-    level = lax.broadcasted_iota(jnp.int32, (NK, NI), 0).astype(F32)
-    turned = NI - 1 - lanes()
-    p1 = [p1_ref[pl.ds(8 * n, 8), :] for n in range(MROWS // 8)]
-    p2 = [p2_ref[pl.ds(8 * n, 8), :] for n in range(MROWS // 8)]
-    south = [jnp.where(even, b, a) for a, b in zip(p1, p2)]
-    north = [jnp.where(is_north, jnp.take_along_axis(b, turned, axis=1), jnp.where(even, a, b)) for a, b in zip(p1, p2)]
-
-    def plane(msg, n):
-        return jnp.concatenate([msg[2 * n], msg[2 * n + 1]], axis=0)
-
-    def wide(row):
-        return jnp.broadcast_to(row, (NK, NI))
-
-    floors = [wide(k_ref[pl.ds(r, 1), :].astype(F32)) for r in ROWS]
-    s_floor = [wide(south[10][1:2]), wide(south[10][0:1])] + floors[0:3]
-    n_floor = floors[3:6] + [wide(north[10][0:1]), wide(north[10][1:2])]
-    last = jnp.where(is_north, 0.5 * (rows_ref[14] - plane(north, 4)), rows_ref[14])
-    merid_ref[...] = jnp.zeros_like(merid_ref)
-    for n in range(2):
-        q = [rows_ref[6 * n + r] for r in range(6)]
-        f0, f1 = edge_fluxes(level, [plane(south, 2 * n + 1), plane(south, 2 * n)] + q[0:3], s_floor, (plane(south, 4), rows_ref[12]))
-        f2, f3 = edge_fluxes(level, q[3:6] + [plane(north, 2 * n), plane(north, 2 * n + 1)], n_floor, (rows_ref[13], last))
-        for side, r, x in ((0, 0, f1 - f0), (0, 1, -f1), (2, 6, f2), (2, 7, f3 - f2)):
-            for k in range(NK):
-                merid_ref[n, side, k, pl.ds(r, 1), :] = x[k : k + 1]
-
-    edge_lanes = (lane < 2) | (lane >= NI - 2)
-
-    def block(b):
-        return pl.ds(pl.multiple_of(b * SOLVE_ROWS, SOLVE_ROWS), SOLVE_ROWS)
-
-    def out_copies(b):
-        at = block(b)
-        return [
-            pltpu.make_async_copy(to_ref.at[:, at], tn_hbm.at[:, at], out_sems.at[0, b]),
-            pltpu.make_async_copy(so_ref.at[:, at], sn_hbm.at[:, at], out_sems.at[1, b]),
-        ]
-
-    def column(b, _):
-        at = block(b)
-        floor = k_ref[at, :]
-        wet = [floor > k for k in range(NK)]
-        star = []
-        for n, (first, ref) in enumerate(((ts_in, ts_ref), (ss_in, ss_ref))):
-            star.append([])
-            for k in range(NK):
-                corrections = []
-                for h in range(SOLVE_ROWS // 8):
-                    c = b * (SOLVE_ROWS // 8) + h
-                    z = pltpu.roll(zonal_ref[n, k % 4], lax.rem(2 * NI - 2 - 4 * (k // 4) - 16 * c, NI), 1)
-                    side = jnp.where(c == 0, 0, jnp.where(c == NB - 1, 2, 1))
-                    corrections.append(jnp.where(edge_lanes, z, 0.0) + merid_ref[n, side, k])
-                x = jnp.where(done_first, first[k, at, :], ref[k, at, :]) - jnp.concatenate(corrections, axis=0)
-                star[n].append(jnp.where(wet[k], x, 0.0))
-        dens = []
-        for k in range(NK):
-            z = LAYER_DEPTH * (k + 0.5)
-            ta = star[0][k] - 10.0
-            sa = star[1][k] - 35.0
-            heat = (-0.5 * THERMAL_COEF * CABBELING_T) * ta - MIXED_COEF * sa - THERMAL_COEF * (1.0 + THERMOBARIC_T * z)
-            salt = (-0.5 * HALINE_COEF * CABBELING_S) * sa + HALINE_COEF * (1.0 - THERMOBARIC_S * z)
-            dens.append(heat * ta + salt * sa)
-        above = None
-        ratio = []
-        values = ([], [])
-        for k in range(NK):
-            if k < NK - 1:
-                below = jnp.where(wet[k + 1], 5.5 - 5.0 * jnp.tanh(dens[k + 1] - dens[k]), 0.0)
-                pivot = 1.0 + below
-            else:
-                below = None
-                pivot = 1.0
-            if k > 0:
-                pivot = pivot + above * (1.0 - ratio[-1])
-            r = pl.reciprocal(pivot, approx=True)
-            r = r * (2.0 - pivot * r)
-            if below is not None:
-                ratio.append(below * r)
-            for n in range(2):
-                x = star[n][k]
-                if k > 0:
-                    x = x + above * values[n][-1]
-                values[n].append(x * r)
-            above = below
-        for n, out in enumerate((to_ref, so_ref)):
-            x = values[n][NK - 1]
-            out[NK - 1, at, :] = jnp.where(wet[NK - 1], x, 0.0)
-            for k in range(NK - 2, -1, -1):
-                x = values[n][k] + ratio[k] * x
-                out[k, at, :] = jnp.where(wet[k], x, 0.0)
-        for c in out_copies(b):
-            c.start()
-        return 0
-
-    lax.fori_loop(0, NJ // SOLVE_ROWS, column, 0)
-    for b in range(NJ // SOLVE_ROWS):
-        for c in out_copies(b):
-            c.wait()
-
-
-def solve(t, s, u, v, w, floor, ts, ss, *edges):
+    def stars(n, k, at):
+        return jnp.where(done_first, (ts_in, ss_in)[n][k, at, :], (ts_ref, ss_ref)[n][k, at, :])
+
+    folded = lax.axis_index("ja") == lax.axis_size("ja") - 1
+    solve_rows(even_row(), folded, t_ref, s_ref, v_ref, k_ref, p2_ref, zonal_ref, stars, (tn_ref, sn_ref), rows_ref, merid_ref)
+
+
+def first_half(t, s, u, v, w, floor, ts, ss, *edges):
     vmem = pl.BlockSpec(memory_space=pltpu.VMEM)
     hbm = pl.BlockSpec(memory_space=pltpu.HBM)
-    field = pltpu.VMEM((NK, NJ, NI), F32)
     w = pltpu.with_memory_space_constraint(w, pltpu.HBM)
     return pl.pallas_call(
-        solve_kernel,
+        first_kernel,
+        out_shape=(pltpu.VMEM((NK, HALF, NI), F32),) * 2
+        + (pltpu.VMEM((NK, NJ, NI), F32),) * 2
+        + (pltpu.VMEM((2, 4, 8, NI), F32),),
+        in_specs=[vmem] * 4 + [hbm] + [vmem] * (3 + len(edges)),
+        out_specs=(vmem,) * 5,
+        scratch_shapes=[pltpu.VMEM((9, NK, NI), F32), pltpu.VMEM((2, NK, 8, NI), F32)] + bulk_scratch(),
+        compiler_params=pltpu.CompilerParams(vmem_limit_bytes=24 * 2**20),
+        cost_estimate=pl.CostEstimate(flops=16_000_000, bytes_accessed=4_000_000, transcendentals=150_000),
+        name="solve_first_half",
+    )(t, s, u, v, w, floor, ts, ss, *edges)
+
+
+def second_kernel(
+    t_ref, s_ref, v_ref, k_ref, ts_in, ss_in, ts_late, ss_late, zonal_ref, tn_ref, sn_ref, p1_ref, tn_hbm, sn_hbm,
+    to_ref, so_ref, rows_ref, merid_ref, sems,
+):
+    south = jnp.logical_not(even_row())
+    other, mine = half_rows(jnp.logical_not(south)), half_rows(south)
+    first = [pltpu.make_async_copy(tn_ref, tn_hbm.at[:, other], sems.at[0]), pltpu.make_async_copy(sn_ref, sn_hbm.at[:, other], sems.at[1])]
+    for c in first:
+        c.start()
+    done_first = bulk_first()
+
+    def stars(n, k, at):
+        return jnp.where(done_first, (ts_in, ss_in)[n][k, at, :], (ts_late, ss_late)[n][k, at, :])
+
+    solve_rows(south, None, t_ref, s_ref, v_ref, k_ref, p1_ref, zonal_ref, stars, (to_ref, so_ref), rows_ref, merid_ref)
+    second = [pltpu.make_async_copy(to_ref, tn_hbm.at[:, mine], sems.at[2]), pltpu.make_async_copy(so_ref, sn_hbm.at[:, mine], sems.at[3])]
+    for c in second:
+        c.start()
+    for c in first + second:
+        c.wait()
+
+
+def second_half(*operands):
+    vmem = pl.BlockSpec(memory_space=pltpu.VMEM)
+    hbm = pl.BlockSpec(memory_space=pltpu.HBM)
+    half = pltpu.VMEM((NK, HALF, NI), F32)
+    return pl.pallas_call(
+        second_kernel,
         out_shape=(jax.ShapeDtypeStruct((NK, NJ, NI), F32),) * 2,
-        in_specs=[vmem] * 4 + [hbm] + [vmem] * (3 + len(edges)),
+        in_specs=[vmem] * len(operands),
         out_specs=(hbm, hbm),
-        scratch_shapes=[field] * 4
-        + [
-            pltpu.VMEM((2, 4, 8, NI), F32),
-            pltpu.VMEM((2, 3, NK, 8, NI), F32),
-            pltpu.VMEM((15, NK, NI), F32),
-            pltpu.SemaphoreType.DMA((2, NB)),
-        ]
-        + bulk_scratch(),
+        scratch_shapes=[
+            half,
+            half,
+            pltpu.VMEM((9, NK, NI), F32),
+            pltpu.VMEM((2, NK, 8, NI), F32),
+            pltpu.SemaphoreType.DMA((4,)),
+        ],
         compiler_params=pltpu.CompilerParams(vmem_limit_bytes=24 * 2**20),
-        cost_estimate=pl.CostEstimate(flops=6_000_000, bytes_accessed=2_500_000, transcendentals=300_000),
-        name="solve_columns",
-    )(t, s, u, v, w, floor, ts, ss, *edges)
+        cost_estimate=pl.CostEstimate(flops=3_000_000, bytes_accessed=2_000_000, transcendentals=150_000),
+        name="solve_second_half",
+    )(*operands)
 
 
 def local(nj, ni, t, s, u, v, w, floor):
@@ -435,7 +470,8 @@
     p2 = lax.ppermute(p2, ("ja", "ia"), second)
     from_west = lax.ppermute(east, "ia", [(i, (i + 1) % ni) for i in range(ni)])
     from_east = lax.ppermute(west, "ia", [((i + 1) % ni, i) for i in range(ni)])
-    return solve(t, s, u, v, w, floor, ts, ss, own, p2, from_west, from_east, p1)
+    tn, sn, ts_late, ss_late, zonal = first_half(t, s, u, v, w, floor, ts, ss, own, from_west, p2, from_east)
+    return second_half(t, s, v, floor, ts, ss, ts_late, ss_late, zonal, tn, sn, p1)
 
 
 def solution(mesh):

time: 28 us -> 26.8 us (0.957)
  the two profiles are of different devices: /device:TPU:127 before, /device:TPU:17 now
where the time goes in v3:
time: 26.8 us; the launch traced here: 26.6 us
  starting transfers between devices  18.6 us (69%)
  Pallas kernels  7.13 us (27%)
  between operations  0.7 us (3%)
    ppermute x1, starting transfers between devices, local(): from_east = lax.ppermute(west, 'ia', [((i + 1) % ni, i) for i in range(ni)])  7.77 us
    pallas_call x1, Pallas kernels, pack(): pl.pallas_call(pack_kernel, out_shape=tuple((pltpu.VMEM(shape, F32) for s...  4.99 us
    ppermute x1, starting transfers between devices, local(): p1 = lax.ppermute(p1, ('ja', 'ia'), first)  3.96 us
    ppermute x1, starting transfers between devices, local(): p2 = lax.ppermute(p2, ('ja', 'ia'), second)  3.96 us
    ppermute x1, starting transfers between devices, local(): from_west = lax.ppermute(east, 'ia', [(i, (i + 1) % ni) for i in range(ni)])  2.91 us
    pallas_call x1, Pallas kernels, second_half(): pl.pallas_call(second_kernel, out_shape=(jax.ShapeDtypeStruct((NK, NJ, NI...  1.46 us
    pallas_call x1, Pallas kernels, first_half(): pl.pallas_call(first_kernel, out_shape=(pltpu.VMEM((NK, HALF, NI), F32),)...  0.68 us
  transfers between devices with their start and end apart: 4, of which 1 were waited for; matrix products, arithmetic and copies ran while one was open for 0% of the time, Pallas kernels for 3%

profile of v3, /device:TPU:17, one launch (start us, length us, event | category | flops | bytes accessed | tf_op | source)
XLA Modules:
  0.0 26.6 jit_solution(16101389319356220010)
XLA Ops:
  0.6 5.0 %pack_edges.1 = (f32[88,128]{1,0:T(8,128)S(1)}, f32[11,8,128]{2,1,0:T(8,128)S(1)}, f32[11,8,128]{2,1,0:T(8,128)S(1)}, f32[88,128]{1,0:T(8,128)S(1)}, f32[21,8,12...) custom-call(f32[16,64,128]{2,1,0:T(8,128)} %t_hbm.1, ...), custom_call_target="tpu_custom_call" | custom-call | tf_op jit(solution)/shard_map/pack_edges/pallas_call | solution.py:232
  5.6 2.9 %collective-permute-start = (f32[11,8,128]{2,1,0:T(8,128)S(1)}, f32[11,8,128]{2,1,0:T(8,128)S(1)}, u32[]{:S(2)}, u32[]{:S(2)}) collective-permute-start(f32[11,8,128]{2,1,0:T(8,128)S(1)} %get-tuple-element.27), channel_id=1, source_target_pairs={{0,1},{1,2},{2,3},{3,4},{4,5},{5,6},{6,7},{7,8},{8,9},{9,10},{10,1... | collective-permute-start | bytes 135176 | tf_op jit(solution)/shard_map/ppermute | solution.py:471
  8.5 4.0 %collective-permute-start.1 = (f32[88,128]{1,0:T(8,128)S(1)}, f32[88,128]{1,0:T(8,128)S(1)}, u32[]{:S(2)}, u32[]{:S(2)}) collective-permute-start(f32[88,128]{1,0:T(8,128)S(1)} %get-tuple-element.28), channel_id=1, source_target_pairs={{32,64},{64,32},{96,128},{128,96},{160,192},{192,160},{224,256},{2... | collective-permute-start | bytes 135176 | tf_op jit(solution)/shard_map/ppermute | solution.py:470
  12.5 7.8 %collective-permute-start.2 = (f32[11,8,128]{2,1,0:T(8,128)S(1)}, f32[11,8,128]{2,1,0:T(8,128)S(1)}, u32[]{:S(2)}, u32[]{:S(2)}) collective-permute-start(f32[11,8,128]{2,1,0:T(8,128)S(1)} %get-tuple-element.29), channel_id=1, source_target_pairs={{1,0},{2,1},{3,2},{4,3},{5,4},{6,5},{7,6},{8,7},{9,8},{10,9},{11,1... | collective-permute-start | bytes 135176 | tf_op jit(solution)/shard_map/ppermute | solution.py:472
  20.3 4.0 %collective-permute-start.3 = (f32[88,128]{1,0:T(8,128)S(1)}, f32[88,128]{1,0:T(8,128)S(1)}, u32[]{:S(2)}, u32[]{:S(2)}) collective-permute-start(f32[88,128]{1,0:T(8,128)S(1)} %get-tuple-element.35), channel_id=1, source_target_pairs={{0,32},{32,0},{64,96},{96,64},{128,160},{160,128},{192,224},{224,1... | collective-permute-start | bytes 135176 | tf_op jit(solution)/shard_map/ppermute | solution.py:469
  24.3 0.0 collective-permute-done.east_ref
  24.3 0.0 collective-permute-done.1.p2_ref
  24.3 0.0 collective-permute-done.2.west_ref
  24.3 0.7 %solve_first_half.1 = (f32[16,32,128]{2,1,0:T(8,128)S(1)}, f32[16,32,128]{2,1,0:T(8,128)S(1)}, f32[16,64,128]{2,1,0:T(8,128)S(1)}, f32[16,64,128]{2,1,0:T(8,128)S(1)}, f32[2,4,8,128]{3,2,1,0:T(8,128)S(1)}) custom-call(f32[16,64,128]{2,1,0:T(8,128)S(1)} %get-tuple-element.19.t_ref, f32[16,64,128]{2,1,0:T(8,128)S(1)} %get-tuple-element.20.s_ref, ...), custom_call_target="tpu_custom_call" | custom-call | flops 16000000 | bytes 4000000 | tf_op jit(solution)/shard_map/solve_first_half/pallas_call | solution.py:401
  25.0 0.1 collective-permute-done.3.p1_ref
  25.1 1.5 %solve_second_half.1 = (f32[16,64,128]{2,1,0:T(8,128)}, f32[16,64,128]{2,1,0:T(8,128)}) custom-call(f32[16,64,128]{2,1,0:T(8,128)S(1)} %get-tuple-element.19.t_ref, f32[16,64,128]{2,1,0:T(8,128)S(1)} %get-tuple-element.20.s_ref, f32[16,64,128]{2,1,0:T(8,128)S(1)} %get-tuple-element.21.v_ref, s32[64,128]{1,0:T(8,128)S(1)} %get-tuple-element.22.k_ref, ...), custom_call_target="tpu_custom_call" | custom-call | flops 3000000 | bytes 2000000 | tf_op jit(solution)/shard_map/solve_second_half/pallas_call | solution.py:441
Async XLA Ops:
  5.6 18.6 %collective-permute-start = (f32[11,8,128]{2,1,0:T(8,128)S(1)}, f32[11,8,128]{2,1,0:T(8,128)S(1)}, u32[]{:S(2)}, u32[]{:S(2)}) collective-permute-start(f32[11,8,128]{2,1,0:T(8,128)S(1)} %get-tuple-element.27), channel_id=1, source_target_pairs={{0,1},{1,2},{2,3},{3,4},{4,5},{5,6},{6,7},{7,8},{8,9},{9,10},{10,1... | collective-permute-start | bytes 135176 | tf_op jit(solution)/shard_map/ppermute | solution.py:471
  8.5 15.7 %collective-permute-start.1 = (f32[88,128]{1,0:T(8,128)S(1)}, f32[88,128]{1,0:T(8,128)S(1)}, u32[]{:S(2)}, u32[]{:S(2)}) collective-permute-start(f32[88,128]{1,0:T(8,128)S(1)} %get-tuple-element.28), channel_id=1, source_target_pairs={{32,64},{64,32},{96,128},{128,96},{160,192},{192,160},{224,256},{2... | collective-permute-start | bytes 135176 | tf_op jit(solution)/shard_map/ppermute | solution.py:470
  12.5 11.8 %collective-permute-start.2 = (f32[11,8,128]{2,1,0:T(8,128)S(1)}, f32[11,8,128]{2,1,0:T(8,128)S(1)}, u32[]{:S(2)}, u32[]{:S(2)}) collective-permute-start(f32[11,8,128]{2,1,0:T(8,128)S(1)} %get-tuple-element.29), channel_id=1, source_target_pairs={{1,0},{2,1},{3,2},{4,3},{5,4},{6,5},{7,6},{8,7},{9,8},{10,9},{11,1... | collective-permute-start | bytes 135176 | tf_op jit(solution)/shard_map/ppermute | solution.py:472
  20.3 4.8 %collective-permute-start.3 = (f32[88,128]{1,0:T(8,128)S(1)}, f32[88,128]{1,0:T(8,128)S(1)}, u32[]{:S(2)}, u32[]{:S(2)}) collective-permute-start(f32[88,128]{1,0:T(8,128)S(1)} %get-tuple-element.35), channel_id=1, source_target_pairs={{0,32},{32,0},{64,96},{96,64},{128,160},{160,128},{192,224},{224,1... | collective-permute-start | bytes 135176 | tf_op jit(solution)/shard_map/ppermute | solution.py:469

commit v4 on v3

--- a/solution.py
+++ b/solution.py
@@ -20,7 +20,8 @@
 NJ = 64
 NI = 128
 NB = NJ // 8
-HALF = NJ // 2
+EDGE = NJ // 2
+LAST = 16
 F32 = jnp.float32
 
 COLS = (-3, -2, -1, 0, 1, 2)
@@ -255,7 +256,7 @@
     return out
 
 
-def solve_rows(south, folded, t_ref, s_ref, v_ref, k_ref, msg_ref, zonal_ref, stars, outs, rows_ref, merid_ref):
+def edge_rows(south, folded, t_ref, s_ref, v_ref, k_ref, msg_ref, rows_ref, merid_ref):
     lane = lanes()
     base = jnp.where(south, 0, NJ - 3)
     for k in range(NK):
@@ -292,9 +293,12 @@
             for k in range(NK):
                 merid_ref[n, k, pl.ds(at_row + i, 1), :] = x[k : k + 1]
 
+
+def solve_rows(start, count, south, k_ref, zonal_ref, merid_ref, stars, outs, first_row):
+    lane = lanes()
     edge_lanes = (lane < 2) | (lane >= NI - 2)
-    half = jnp.where(south, 0, 1)
-    at = half_rows(south)
+    at = pl.ds(pl.multiple_of(start, 8), count)
+    to = pl.ds(pl.multiple_of(start - first_row, 8), count)
     floor = k_ref[at, :]
     wet = [floor > k for k in range(NK)]
     star = []
@@ -302,14 +306,14 @@
         star.append([])
         for k in range(NK):
             corrections = []
-            for h in range(HALF // 8):
-                c = half * (HALF // 8) + h
+            for h in range(count // 8):
+                c = start // 8 + h
                 z = pltpu.roll(zonal_ref[n, k % 4], lax.rem(2 * NI - 2 - 4 * (k // 4) - 16 * c, NI), 1)
                 z = jnp.where(edge_lanes, z, 0.0)
-                if h == 0:
-                    z = z + jnp.where(south, merid_ref[n, k], 0.0)
-                if h == HALF // 8 - 1:
-                    z = z + jnp.where(south, 0.0, merid_ref[n, k])
+                if merid_ref is not None and count == 8:
+                    z = z + merid_ref[n, k]
+                elif merid_ref is not None and h in (0, count // 8 - 1):
+                    z = z + jnp.where(south if h == 0 else jnp.logical_not(south), merid_ref[n, k], 0.0)
                 corrections.append(z)
             star[n].append(jnp.where(wet[k], stars(n, k, at) - jnp.concatenate(corrections, axis=0), 0.0))
     dens = []
@@ -344,14 +348,10 @@
         above = below
     for n in range(2):
         x = values[n][NK - 1]
-        outs[n][NK - 1] = jnp.where(wet[NK - 1], x, 0.0)
+        outs[n][NK - 1, to, :] = jnp.where(wet[NK - 1], x, 0.0)
         for k in range(NK - 2, -1, -1):
             x = values[n][k] + ratio[k] * x
-            outs[n][k] = jnp.where(wet[k], x, 0.0)
-
-
-def half_rows(south):
-    return pl.ds(pl.multiple_of(jnp.where(south, 0, HALF), HALF), HALF)
+            outs[n][k, to, :] = jnp.where(wet[k], x, 0.0)
 
 
 def even_row():
@@ -391,16 +391,21 @@
         return jnp.where(done_first, (ts_in, ss_in)[n][k, at, :], (ts_ref, ss_ref)[n][k, at, :])
 
     folded = lax.axis_index("ja") == lax.axis_size("ja") - 1
-    solve_rows(even_row(), folded, t_ref, s_ref, v_ref, k_ref, p2_ref, zonal_ref, stars, (tn_ref, sn_ref), rows_ref, merid_ref)
-
-
-def first_half(t, s, u, v, w, floor, ts, ss, *edges):
+    south = even_row()
+    edge_rows(south, folded, t_ref, s_ref, v_ref, k_ref, p2_ref, rows_ref, merid_ref)
+    base = jnp.where(south, 0, LAST)
+    outs = (tn_ref, sn_ref)
+    solve_rows(jnp.where(south, 0, NJ - EDGE), EDGE, south, k_ref, zonal_ref, merid_ref, stars, outs, base)
+    solve_rows(jnp.where(south, EDGE, LAST), NJ - EDGE - LAST, south, k_ref, zonal_ref, None, stars, outs, base)
+
+
+def most_rows(t, s, u, v, w, floor, ts, ss, *edges):
     vmem = pl.BlockSpec(memory_space=pltpu.VMEM)
     hbm = pl.BlockSpec(memory_space=pltpu.HBM)
     w = pltpu.with_memory_space_constraint(w, pltpu.HBM)
     return pl.pallas_call(
         first_kernel,
-        out_shape=(pltpu.VMEM((NK, HALF, NI), F32),) * 2
+        out_shape=(pltpu.VMEM((NK, NJ - LAST, NI), F32),) * 2
         + (pltpu.VMEM((NK, NJ, NI), F32),) * 2
         + (pltpu.VMEM((2, 4, 8, NI), F32),),
         in_specs=[vmem] * 4 + [hbm] + [vmem] * (3 + len(edges)),
@@ -408,7 +413,7 @@
         scratch_shapes=[pltpu.VMEM((9, NK, NI), F32), pltpu.VMEM((2, NK, 8, NI), F32)] + bulk_scratch(),
         compiler_params=pltpu.CompilerParams(vmem_limit_bytes=24 * 2**20),
         cost_estimate=pl.CostEstimate(flops=16_000_000, bytes_accessed=4_000_000, transcendentals=150_000),
-        name="solve_first_half",
+        name="solve_most_rows",
     )(t, s, u, v, w, floor, ts, ss, *edges)
 
 
@@ -417,7 +422,9 @@
     to_ref, so_ref, rows_ref, merid_ref, sems,
 ):
     south = jnp.logical_not(even_row())
-    other, mine = half_rows(jnp.logical_not(south)), half_rows(south)
+    other = pl.ds(pl.multiple_of(jnp.where(south, LAST, 0), 8), NJ - LAST)
+    start = jnp.where(south, 0, NJ - LAST)
+    mine = pl.ds(pl.multiple_of(start, 8), LAST)
     first = [pltpu.make_async_copy(tn_ref, tn_hbm.at[:, other], sems.at[0]), pltpu.make_async_copy(sn_ref, sn_hbm.at[:, other], sems.at[1])]
     for c in first:
         c.start()
@@ -426,7 +433,8 @@
     def stars(n, k, at):
         return jnp.where(done_first, (ts_in, ss_in)[n][k, at, :], (ts_late, ss_late)[n][k, at, :])
 
-    solve_rows(south, None, t_ref, s_ref, v_ref, k_ref, p1_ref, zonal_ref, stars, (to_ref, so_ref), rows_ref, merid_ref)
+    edge_rows(south, None, t_ref, s_ref, v_ref, k_ref, p1_ref, rows_ref, merid_ref)
+    solve_rows(start, LAST, south, k_ref, zonal_ref, merid_ref, stars, (to_ref, so_ref), start)
     second = [pltpu.make_async_copy(to_ref, tn_hbm.at[:, mine], sems.at[2]), pltpu.make_async_copy(so_ref, sn_hbm.at[:, mine], sems.at[3])]
     for c in second:
         c.start()
@@ -434,25 +442,25 @@
         c.wait()
 
 
-def second_half(*operands):
+def last_rows(*operands):
     vmem = pl.BlockSpec(memory_space=pltpu.VMEM)
     hbm = pl.BlockSpec(memory_space=pltpu.HBM)
-    half = pltpu.VMEM((NK, HALF, NI), F32)
+    edge = pltpu.VMEM((NK, LAST, NI), F32)
     return pl.pallas_call(
         second_kernel,
         out_shape=(jax.ShapeDtypeStruct((NK, NJ, NI), F32),) * 2,
         in_specs=[vmem] * len(operands),
         out_specs=(hbm, hbm),
         scratch_shapes=[
-            half,
-            half,
+            edge,
+            edge,
             pltpu.VMEM((9, NK, NI), F32),
             pltpu.VMEM((2, NK, 8, NI), F32),
             pltpu.SemaphoreType.DMA((4,)),
         ],
         compiler_params=pltpu.CompilerParams(vmem_limit_bytes=24 * 2**20),
         cost_estimate=pl.CostEstimate(flops=3_000_000, bytes_accessed=2_000_000, transcendentals=150_000),
-        name="solve_second_half",
+        name="solve_edge_rows",
     )(*operands)
 
 
@@ -470,8 +478,8 @@
     p2 = lax.ppermute(p2, ("ja", "ia"), second)
     from_west = lax.ppermute(east, "ia", [(i, (i + 1) % ni) for i in range(ni)])
     from_east = lax.ppermute(west, "ia", [((i + 1) % ni, i) for i in range(ni)])
-    tn, sn, ts_late, ss_late, zonal = first_half(t, s, u, v, w, floor, ts, ss, own, from_west, p2, from_east)
-    return second_half(t, s, v, floor, ts, ss, ts_late, ss_late, zonal, tn, sn, p1)
+    tn, sn, ts_late, ss_late, zonal = most_rows(t, s, u, v, w, floor, ts, ss, own, from_west, p2, from_east)
+    return last_rows(t, s, v, floor, ts, ss, ts_late, ss_late, zonal, tn, sn, p1)
 
 
 def solution(mesh):

time: 26.8 us -> 26.7 us (level)
  transfers between devices with their start and end apart: 4 -> 4, of which waited for: 1 -> 0; matrix products, arithmetic and copies ran while one was open for 0% -> 0% of each run, Pallas kernels for 3% -> 3%
where the time goes in v4:
time: 26.7 us; the launch traced here: 26.5 us
  starting transfers between devices  18.6 us (70%)
  Pallas kernels  7.15 us (27%)
  between operations  0.71 us (3%)
    ppermute x1, starting transfers between devices, local(): from_east = lax.ppermute(west, 'ia', [((i + 1) % ni, i) for i in range(ni)])  7.77 us
    pallas_call x1, Pallas kernels, pack(): pl.pallas_call(pack_kernel, out_shape=tuple((pltpu.VMEM(shape, F32) for s...  4.99 us
    ppermute x1, starting transfers between devices, local(): p1 = lax.ppermute(p1, ('ja', 'ia'), first)  3.96 us
    ppermute x1, starting transfers between devices, local(): p2 = lax.ppermute(p2, ('ja', 'ia'), second)  3.96 us
    ppermute x1, starting transfers between devices, local(): from_west = lax.ppermute(east, 'ia', [(i, (i + 1) % ni) for i in range(ni)])  2.91 us
    pallas_call x1, Pallas kernels, last_rows(): pl.pallas_call(second_kernel, out_shape=(jax.ShapeDtypeStruct((NK, NJ, NI...  1.28 us
    pallas_call x1, Pallas kernels, most_rows(): pl.pallas_call(first_kernel, out_shape=(pltpu.VMEM((NK, NJ - LAST, NI), F...  0.88 us
  transfers between devices with their start and end apart: 4, of which 0 were waited for; matrix products, arithmetic and copies ran while one was open for 0% of the time, Pallas kernels for 3%

profile of v4, /device:TPU:17, one launch (start us, length us, event | category | flops | bytes accessed | tf_op | source)
XLA Modules:
  0.0 26.5 jit_solution(6403243027046371923)
XLA Ops:
  0.6 5.0 %pack_edges.1 = (f32[88,128]{1,0:T(8,128)S(1)}, f32[11,8,128]{2,1,0:T(8,128)S(1)}, f32[11,8,128]{2,1,0:T(8,128)S(1)}, f32[88,128]{1,0:T(8,128)S(1)}, f32[21,8,12...) custom-call(f32[16,64,128]{2,1,0:T(8,128)} %t_hbm.1, ...), custom_call_target="tpu_custom_call" | custom-call | tf_op jit(solution)/shard_map/pack_edges/pallas_call | solution.py:233
  5.6 2.9 %collective-permute-start = (f32[11,8,128]{2,1,0:T(8,128)S(1)}, f32[11,8,128]{2,1,0:T(8,128)S(1)}, u32[]{:S(2)}, u32[]{:S(2)}) collective-permute-start(f32[11,8,128]{2,1,0:T(8,128)S(1)} %get-tuple-element.27), channel_id=1, source_target_pairs={{0,1},{1,2},{2,3},{3,4},{4,5},{5,6},{6,7},{7,8},{8,9},{9,10},{10,1... | collective-permute-start | bytes 135176 | tf_op jit(solution)/shard_map/ppermute | solution.py:479
  8.5 4.0 %collective-permute-start.1 = (f32[88,128]{1,0:T(8,128)S(1)}, f32[88,128]{1,0:T(8,128)S(1)}, u32[]{:S(2)}, u32[]{:S(2)}) collective-permute-start(f32[88,128]{1,0:T(8,128)S(1)} %get-tuple-element.28), channel_id=1, source_target_pairs={{32,64},{64,32},{96,128},{128,96},{160,192},{192,160},{224,256},{2... | collective-permute-start | bytes 135176 | tf_op jit(solution)/shard_map/ppermute | solution.py:478
  12.5 7.8 %collective-permute-start.2 = (f32[11,8,128]{2,1,0:T(8,128)S(1)}, f32[11,8,128]{2,1,0:T(8,128)S(1)}, u32[]{:S(2)}, u32[]{:S(2)}) collective-permute-start(f32[11,8,128]{2,1,0:T(8,128)S(1)} %get-tuple-element.29), channel_id=1, source_target_pairs={{1,0},{2,1},{3,2},{4,3},{5,4},{6,5},{7,6},{8,7},{9,8},{10,9},{11,1... | collective-permute-start | bytes 135176 | tf_op jit(solution)/shard_map/ppermute | solution.py:480
  20.3 4.0 %collective-permute-start.3 = (f32[88,128]{1,0:T(8,128)S(1)}, f32[88,128]{1,0:T(8,128)S(1)}, u32[]{:S(2)}, u32[]{:S(2)}) collective-permute-start(f32[88,128]{1,0:T(8,128)S(1)} %get-tuple-element.35), channel_id=1, source_target_pairs={{0,32},{32,0},{64,96},{96,64},{128,160},{160,128},{192,224},{224,1... | collective-permute-start | bytes 135176 | tf_op jit(solution)/shard_map/ppermute | solution.py:477
  24.3 0.0 collective-permute-done.east_ref
  24.3 0.0 collective-permute-done.1.p2_ref
  24.3 0.0 collective-permute-done.2.west_ref
  24.3 0.9 %solve_most_rows.1 = (f32[16,48,128]{2,1,0:T(8,128)S(1)}, f32[16,48,128]{2,1,0:T(8,128)S(1)}, f32[16,64,128]{2,1,0:T(8,128)S(1)}, f32[16,64,128]{2,1,0:T(8,128)S(1)}, f32[2,4,8,128]{3,2,1,0:T(8,128)S(1)}) custom-call(f32[16,64,128]{2,1,0:T(8,128)S(1)} %get-tuple-element.19.t_ref, f32[16,64,128]{2,1,0:T(8,128)S(1)} %get-tuple-element.20.s_ref, ...), custom_call_target="tpu_custom_call" | custom-call | flops 16000000 | bytes 4000000 | tf_op jit(solution)/shard_map/solve_most_rows/pallas_call | solution.py:406
  25.2 0.0 collective-permute-done.3.p1_ref
  25.2 1.3 %solve_edge_rows.1 = (f32[16,64,128]{2,1,0:T(8,128)}, f32[16,64,128]{2,1,0:T(8,128)}) custom-call(f32[16,64,128]{2,1,0:T(8,128)S(1)} %get-tuple-element.19.t_ref, f32[16,64,128]{2,1,0:T(8,128)S(1)} %get-tuple-element.20.s_ref, f32[16,64,128]{2,1,0:T(8,128)S(1)} %get-tuple-element.21.v_ref, s32[64,128]{1,0:T(8,128)S(1)} %get-tuple-element.22.k_ref, ...), custom_call_target="tpu_custom_call" | custom-call | flops 3000000 | bytes 2000000 | tf_op jit(solution)/shard_map/solve_edge_rows/pallas_call | solution.py:449
Async XLA Ops:
  5.6 18.6 %collective-permute-start = (f32[11,8,128]{2,1,0:T(8,128)S(1)}, f32[11,8,128]{2,1,0:T(8,128)S(1)}, u32[]{:S(2)}, u32[]{:S(2)}) collective-permute-start(f32[11,8,128]{2,1,0:T(8,128)S(1)} %get-tuple-element.27), channel_id=1, source_target_pairs={{0,1},{1,2},{2,3},{3,4},{4,5},{5,6},{6,7},{7,8},{8,9},{9,10},{10,1... | collective-permute-start | bytes 135176 | tf_op jit(solution)/shard_map/ppermute | solution.py:479
  8.5 15.7 %collective-permute-start.1 = (f32[88,128]{1,0:T(8,128)S(1)}, f32[88,128]{1,0:T(8,128)S(1)}, u32[]{:S(2)}, u32[]{:S(2)}) collective-permute-start(f32[88,128]{1,0:T(8,128)S(1)} %get-tuple-element.28), channel_id=1, source_target_pairs={{32,64},{64,32},{96,128},{128,96},{160,192},{192,160},{224,256},{2... | collective-permute-start | bytes 135176 | tf_op jit(solution)/shard_map/ppermute | solution.py:478
  12.5 11.8 %collective-permute-start.2 = (f32[11,8,128]{2,1,0:T(8,128)S(1)}, f32[11,8,128]{2,1,0:T(8,128)S(1)}, u32[]{:S(2)}, u32[]{:S(2)}) collective-permute-start(f32[11,8,128]{2,1,0:T(8,128)S(1)} %get-tuple-element.29), channel_id=1, source_target_pairs={{1,0},{2,1},{3,2},{4,3},{5,4},{6,5},{7,6},{8,7},{9,8},{10,9},{11,1... | collective-permute-start | bytes 135176 | tf_op jit(solution)/shard_map/ppermute | solution.py:480
  20.3 4.9 %collective-permute-start.3 = (f32[88,128]{1,0:T(8,128)S(1)}, f32[88,128]{1,0:T(8,128)S(1)}, u32[]{:S(2)}, u32[]{:S(2)}) collective-permute-start(f32[88,128]{1,0:T(8,128)S(1)} %get-tuple-element.35), channel_id=1, source_target_pairs={{0,32},{32,0},{64,96},{96,64},{128,160},{160,128},{192,224},{224,1... | collective-permute-start | bytes 135176 | tf_op jit(solution)/shard_map/ppermute | solution.py:477

commit v5 on v4

--- a/solution.py
+++ b/solution.py
@@ -148,7 +148,7 @@
     t_hbm, s_hbm, u_hbm, v_hbm, w_hbm, k_hbm, p2_ref, east_ref, west_ref, p1_ref, own_ref,
     t_ref, s_ref, u_ref, v_ref, k_ref, ts_ref, ss_ref, sems, *scratch,
 ):
-    chunks = 4
+    chunks = 2
     per = NK // chunks
     copies = []
     for c in range(chunks):

time: 26.7 us -> 26.6 us (level)
  no operation moved by 1% of the time
where the time goes in v5:
time: 26.6 us; the launch traced here: 26.4 us
  starting transfers between devices  18.6 us (70%)
  Pallas kernels  7.09 us (27%)
  between operations  0.71 us (3%)
    ppermute x1, starting transfers between devices, local(): from_east = lax.ppermute(west, 'ia', [((i + 1) % ni, i) for i in range(ni)])  7.78 us
    pallas_call x1, Pallas kernels, pack(): pl.pallas_call(pack_kernel, out_shape=tuple((pltpu.VMEM(shape, F32) for s...  4.92 us
    ppermute x1, starting transfers between devices, local(): p2 = lax.ppermute(p2, ('ja', 'ia'), second)  3.96 us
    ppermute x1, starting transfers between devices, local(): p1 = lax.ppermute(p1, ('ja', 'ia'), first)  3.96 us
    ppermute x1, starting transfers between devices, local(): from_west = lax.ppermute(east, 'ia', [(i, (i + 1) % ni) for i in range(ni)])  2.91 us
    pallas_call x1, Pallas kernels, last_rows(): pl.pallas_call(second_kernel, out_shape=(jax.ShapeDtypeStruct((NK, NJ, NI...  1.28 us
    pallas_call x1, Pallas kernels, most_rows(): pl.pallas_call(first_kernel, out_shape=(pltpu.VMEM((NK, NJ - LAST, NI), F...  0.88 us
  transfers between devices with their start and end apart: 4, of which 0 were waited for; matrix products, arithmetic and copies ran while one was open for 0% of the time, Pallas kernels for 3%

profile of v5, /device:TPU:17, one launch (start us, length us, event | category | flops | bytes accessed | tf_op | source)
XLA Modules:
  0.0 26.4 jit_solution(708100643526113679)
XLA Ops:
  0.6 4.9 %pack_edges.1 = (f32[88,128]{1,0:T(8,128)S(1)}, f32[11,8,128]{2,1,0:T(8,128)S(1)}, f32[11,8,128]{2,1,0:T(8,128)S(1)}, f32[88,128]{1,0:T(8,128)S(1)}, f32[21,8,12...) custom-call(f32[16,64,128]{2,1,0:T(8,128)} %t_hbm.1, ...), custom_call_target="tpu_custom_call" | custom-call | tf_op jit(solution)/shard_map/pack_edges/pallas_call | solution.py:233
  5.6 2.9 %collective-permute-start = (f32[11,8,128]{2,1,0:T(8,128)S(1)}, f32[11,8,128]{2,1,0:T(8,128)S(1)}, u32[]{:S(2)}, u32[]{:S(2)}) collective-permute-start(f32[11,8,128]{2,1,0:T(8,128)S(1)} %get-tuple-element.27), channel_id=1, source_target_pairs={{0,1},{1,2},{2,3},{3,4},{4,5},{5,6},{6,7},{7,8},{8,9},{9,10},{10,1... | collective-permute-start | bytes 135176 | tf_op jit(solution)/shard_map/ppermute | solution.py:479
  8.5 4.0 %collective-permute-start.1 = (f32[88,128]{1,0:T(8,128)S(1)}, f32[88,128]{1,0:T(8,128)S(1)}, u32[]{:S(2)}, u32[]{:S(2)}) collective-permute-start(f32[88,128]{1,0:T(8,128)S(1)} %get-tuple-element.28), channel_id=1, source_target_pairs={{32,64},{64,32},{96,128},{128,96},{160,192},{192,160},{224,256},{2... | collective-permute-start | bytes 135176 | tf_op jit(solution)/shard_map/ppermute | solution.py:478
  12.4 7.8 %collective-permute-start.2 = (f32[11,8,128]{2,1,0:T(8,128)S(1)}, f32[11,8,128]{2,1,0:T(8,128)S(1)}, u32[]{:S(2)}, u32[]{:S(2)}) collective-permute-start(f32[11,8,128]{2,1,0:T(8,128)S(1)} %get-tuple-element.29), channel_id=1, source_target_pairs={{1,0},{2,1},{3,2},{4,3},{5,4},{6,5},{7,6},{8,7},{9,8},{10,9},{11,1... | collective-permute-start | bytes 135176 | tf_op jit(solution)/shard_map/ppermute | solution.py:480
  20.2 4.0 %collective-permute-start.3 = (f32[88,128]{1,0:T(8,128)S(1)}, f32[88,128]{1,0:T(8,128)S(1)}, u32[]{:S(2)}, u32[]{:S(2)}) collective-permute-start(f32[88,128]{1,0:T(8,128)S(1)} %get-tuple-element.35), channel_id=1, source_target_pairs={{0,32},{32,0},{64,96},{96,64},{128,160},{160,128},{192,224},{224,1... | collective-permute-start | bytes 135176 | tf_op jit(solution)/shard_map/ppermute | solution.py:477
  24.2 0.0 collective-permute-done.east_ref
  24.2 0.0 collective-permute-done.1.p2_ref
  24.2 0.0 collective-permute-done.2.west_ref
  24.2 0.9 %solve_most_rows.1 = (f32[16,48,128]{2,1,0:T(8,128)S(1)}, f32[16,48,128]{2,1,0:T(8,128)S(1)}, f32[16,64,128]{2,1,0:T(8,128)S(1)}, f32[16,64,128]{2,1,0:T(8,128)S(1)}, f32[2,4,8,128]{3,2,1,0:T(8,128)S(1)}) custom-call(f32[16,64,128]{2,1,0:T(8,128)S(1)} %get-tuple-element.19.t_ref, f32[16,64,128]{2,1,0:T(8,128)S(1)} %get-tuple-element.20.s_ref, ...), custom_call_target="tpu_custom_call" | custom-call | flops 16000000 | bytes 4000000 | tf_op jit(solution)/shard_map/solve_most_rows/pallas_call | solution.py:406
  25.1 0.0 collective-permute-done.3.p1_ref
  25.1 1.3 %solve_edge_rows.1 = (f32[16,64,128]{2,1,0:T(8,128)}, f32[16,64,128]{2,1,0:T(8,128)}) custom-call(f32[16,64,128]{2,1,0:T(8,128)S(1)} %get-tuple-element.19.t_ref, f32[16,64,128]{2,1,0:T(8,128)S(1)} %get-tuple-element.20.s_ref, f32[16,64,128]{2,1,0:T(8,128)S(1)} %get-tuple-element.21.v_ref, s32[64,128]{1,0:T(8,128)S(1)} %get-tuple-element.22.k_ref, ...), custom_call_target="tpu_custom_call" | custom-call | flops 3000000 | bytes 2000000 | tf_op jit(solution)/shard_map/solve_edge_rows/pallas_call | solution.py:449
Async XLA Ops:
  5.6 18.6 %collective-permute-start = (f32[11,8,128]{2,1,0:T(8,128)S(1)}, f32[11,8,128]{2,1,0:T(8,128)S(1)}, u32[]{:S(2)}, u32[]{:S(2)}) collective-permute-start(f32[11,8,128]{2,1,0:T(8,128)S(1)} %get-tuple-element.27), channel_id=1, source_target_pairs={{0,1},{1,2},{2,3},{3,4},{4,5},{5,6},{6,7},{7,8},{8,9},{9,10},{10,1... | collective-permute-start | bytes 135176 | tf_op jit(solution)/shard_map/ppermute | solution.py:479
  8.5 15.7 %collective-permute-start.1 = (f32[88,128]{1,0:T(8,128)S(1)}, f32[88,128]{1,0:T(8,128)S(1)}, u32[]{:S(2)}, u32[]{:S(2)}) collective-permute-start(f32[88,128]{1,0:T(8,128)S(1)} %get-tuple-element.28), channel_id=1, source_target_pairs={{32,64},{64,32},{96,128},{128,96},{160,192},{192,160},{224,256},{2... | collective-permute-start | bytes 135176 | tf_op jit(solution)/shard_map/ppermute | solution.py:478
  12.4 11.8 %collective-permute-start.2 = (f32[11,8,128]{2,1,0:T(8,128)S(1)}, f32[11,8,128]{2,1,0:T(8,128)S(1)}, u32[]{:S(2)}, u32[]{:S(2)}) collective-permute-start(f32[11,8,128]{2,1,0:T(8,128)S(1)} %get-tuple-element.29), channel_id=1, source_target_pairs={{1,0},{2,1},{3,2},{4,3},{5,4},{6,5},{7,6},{8,7},{9,8},{10,9},{11,1... | collective-permute-start | bytes 135176 | tf_op jit(solution)/shard_map/ppermute | solution.py:480
  20.2 4.9 %collective-permute-start.3 = (f32[88,128]{1,0:T(8,128)S(1)}, f32[88,128]{1,0:T(8,128)S(1)}, u32[]{:S(2)}, u32[]{:S(2)}) collective-permute-start(f32[88,128]{1,0:T(8,128)S(1)} %get-tuple-element.35), channel_id=1, source_target_pairs={{0,32},{32,0},{64,96},{96,64},{128,160},{160,128},{192,224},{224,1... | collective-permute-start | bytes 135176 | tf_op jit(solution)/shard_map/ppermute | solution.py:477
